TPU v7x, 32 devices: a whole 2x2x4 slice. The times are simulated.
32 devices in a mesh: dp: 16 (over z, y, core), ctx: 2 (over x).
Axes of the slice: x: 2, y: 2, z: 4, core: 2. Of those that a mesh axis runs over, the one named last changes fastest.
Arguments:
- frames: bfloat16 [16, 1024, 1280], P('dp', 'ctx'), may hold values from -6 to 6
- conv_taps: float32 [31, 1280], replicated, may hold values from -1 to 1
- conv_gain: float32 [1280], replicated, may hold values from 0.1 to 1.9
- w_kv: bfloat16 [1280, 2560], P('dp'), may hold values from -0.15625 to 0.15625
- queries: bfloat16 [16, 32, 1280], P('dp', 'ctx'), may hold values from -6 to 6
- out_grad: bfloat16 [16, 32, 1280], P('dp', 'ctx'), may hold values from -6 to 6
- frame_len: int32 [16], P('dp'), may hold values from 256 to 1024
- token_len: int32 [16], P('dp'), may hold values from 8 to 32
Outputs:
- frames_grad: bfloat16 [16, 1024, 1280], P('dp', 'ctx')
- taps_grad: float32 [31, 1280], replicated
- gain_grad: float32 [1280], replicated
- w_kv_grad: float32 [1280, 2560], P('dp')
- queries_grad: bfloat16 [16, 32, 1280], P('dp', 'ctx')
Inputs may be any that keep to these rules, and one draw needn't show every extreme that they name: frames at positions of frame_len[b] or beyond are padding of utterance b. Tokens at positions of token_len[b] or beyond are padding of utterance b.
All inputs are finite; a program needn't handle non-finite values.
Results may differ from a plain program's by a relative error of at most 0.012.
Values may be sent and summed in bfloat16 or wider, within the bound.
A program may use at most 128 MiB of HBM per device.

v0:
```python
import jax
import jax.numpy as jnp
from jax import lax
from jax.sharding import PartitionSpec as P

HEADS = 20


def padded_2(block, sides, width):
    for axis, dim in sides:
        count = lax.axis_size(axis)
        forward = [(i, i + 1) for i in range(count - 1)]
        backward = [(target, source) for source, target in forward]
        low = lax.ppermute(
            lax.slice_in_dim(block, block.shape[dim] - width, None, axis=dim), axis, forward
        )
        high = lax.ppermute(lax.slice_in_dim(block, 0, width, axis=dim), axis, backward)
        block = jnp.concatenate([low, block, high], axis=dim)
    return block


def shifted(value, axis, steps):
    count = lax.axis_size(axis)
    pairs = [(source, (source + steps) % count) for source in range(count)]
    return lax.ppermute(value, axis, pairs)


def conv_time(padded, conv_taps, length):
    total = jnp.zeros((length, padded.shape[1]), jnp.float32)
    for tap_idx in range(conv_taps.shape[0]):
        total = total + conv_taps[tap_idx] * padded[tap_idx : tap_idx + length].astype(jnp.float32)
    return total


def silu_slope(gated):
    sigma = jax.nn.sigmoid(gated)
    return sigma * (1.0 + gated * (1.0 - sigma))


def forward_part(query_block, key_block, value_block, live_mask, head_count):
    row_count = query_block.shape[0]
    frame_count = key_block.shape[0]
    q_heads = query_block.reshape(row_count, head_count, -1)
    k_heads = key_block.reshape(frame_count, head_count, -1)
    v_heads = value_block.reshape(frame_count, head_count, -1)
    scale = q_heads.shape[2] ** (-0.5)
    exp_scores = (
        jnp.exp(
            jnp.einsum("thd,fhd->htf", q_heads, k_heads, preferred_element_type=jnp.float32) * scale
        )
        * live_mask
    )
    totals = jnp.sum(exp_scores, axis=2).T
    weighted = jnp.einsum(
        "htf,fhd->thd", exp_scores.astype(jnp.bfloat16), v_heads, preferred_element_type=jnp.float32
    )
    return (weighted.reshape(row_count, -1), totals)


def backward_part(
    query_block, grad_block, totals, delta_rows, key_block, value_block, live_mask, head_count
):
    row_count = query_block.shape[0]
    frame_count = key_block.shape[0]
    q_heads = query_block.reshape(row_count, head_count, -1)
    g_heads = grad_block.reshape(row_count, head_count, -1)
    k_heads = key_block.reshape(frame_count, head_count, -1)
    v_heads = value_block.reshape(frame_count, head_count, -1)
    scale = q_heads.shape[2] ** (-0.5)
    exp_scores = (
        jnp.exp(
            jnp.einsum("thd,fhd->htf", q_heads, k_heads, preferred_element_type=jnp.float32) * scale
        )
        * live_mask
    )
    attn_prob = exp_scores / totals.T[:, :, None]
    d_prob = jnp.einsum("thd,fhd->htf", g_heads, v_heads, preferred_element_type=jnp.float32)
    d_score = (attn_prob * (d_prob - delta_rows.T[:, :, None])).astype(jnp.bfloat16)
    query_part = jnp.einsum(
        "htf,fhd->thd", d_score, k_heads, preferred_element_type=jnp.float32
    ).reshape(row_count, -1)
    key_part = jnp.einsum(
        "htf,thd->fhd", d_score, q_heads, preferred_element_type=jnp.float32
    ).reshape(frame_count, -1)
    value_part = jnp.einsum(
        "htf,thd->fhd", attn_prob.astype(jnp.bfloat16), g_heads, preferred_element_type=jnp.float32
    ).reshape(frame_count, -1)
    return (query_part, key_part, value_part)


def row_delta(weighted, totals, grad_block):
    row_count = weighted.shape[0]
    head_count = totals.shape[1]
    head_dim = weighted.shape[1] // head_count
    attended = weighted / jnp.repeat(totals, head_dim, axis=1)
    return jnp.sum(
        (grad_block.astype(jnp.float32) * attended).reshape(row_count, head_count, head_dim), axis=2
    )


def per_device(frames, conv_taps, conv_gain, w_kv, queries, out_grad, frame_len, token_len):
    cycle_size = lax.axis_size("ctx")
    cycle_pos = lax.axis_index("ctx")
    length = frames.shape[1]
    model_width = frames.shape[2]
    tokens = queries.shape[1]
    tap_count = conv_taps.shape[0]
    rim_width = tap_count // 2
    scale = (model_width // HEADS) ** (-0.5)
    padded = padded_2(frames, (("ctx", 1),), rim_width)[0]
    conv_out = conv_time(padded, conv_taps, length)
    gated = conv_gain * conv_out
    encoded = (frames[0].astype(jnp.float32) + jax.nn.silu(gated)).astype(jnp.bfloat16)
    w_full = lax.all_gather(w_kv, "dp", axis=0, tiled=True)
    key_values = jnp.dot(encoded, w_full, preferred_element_type=jnp.float32).astype(jnp.bfloat16)
    key_block = key_values[:, :model_width]
    value_block = key_values[:, model_width:]
    frame_pos = cycle_pos * length + jnp.arange(length)
    live_mask = (frame_pos < frame_len[0]).astype(jnp.float32)
    token_pos = cycle_pos * tokens + jnp.arange(tokens)
    grad_block = out_grad[0] * (token_pos < token_len[0]).astype(jnp.bfloat16)[:, None]
    query_block = queries[0]

    def forward_tile(visitor, keys_part, values_part, head_count):
        return forward_part(visitor, keys_part, values_part, live_mask, head_count)

    def backward_tile(
        visitor, visit_grad, visit_totals, visit_delta, keys_part, values_part, head_count
    ):
        return backward_part(
            visitor,
            visit_grad,
            visit_totals,
            visit_delta,
            keys_part,
            values_part,
            live_mask,
            head_count,
        )

    def forward_turn(turn_idx, carried):
        visitor, weighted, totals = carried
        part_sum, part_total = forward_tile(visitor, key_block, value_block, HEADS)
        visitor = shifted(visitor, "ctx", 1)
        weighted, totals = shifted((weighted + part_sum, totals + part_total), "ctx", 1)
        return (visitor, weighted, totals)

    first_state = (
        query_block,
        jnp.zeros((tokens, model_width), jnp.float32),
        jnp.zeros((tokens, HEADS), jnp.float32),
    )
    first_out = lax.fori_loop(0, cycle_size, forward_turn, first_state)
    totals = first_out[2]
    delta_rows = row_delta(first_out[1], totals, grad_block)

    def backward_turn(turn_idx, carried):
        visitor, visit_grad, visit_totals, visit_delta, query_acc, key_acc, value_acc = carried
        part_query, part_key, part_value = backward_tile(
            visitor, visit_grad, visit_totals, visit_delta, key_block, value_block, HEADS
        )
        visitor, visit_grad = shifted((visitor, visit_grad), "ctx", 1)
        visit_totals, visit_delta, query_acc = shifted(
            (visit_totals, visit_delta, query_acc + part_query), "ctx", 1
        )
        return (
            visitor,
            visit_grad,
            visit_totals,
            visit_delta,
            query_acc,
            key_acc + part_key,
            value_acc + part_value,
        )

    second_state = (
        query_block,
        grad_block,
        totals,
        delta_rows,
        jnp.zeros((tokens, model_width), jnp.float32),
        jnp.zeros((length, model_width), jnp.float32),
        jnp.zeros((length, model_width), jnp.float32),
    )
    second_out = lax.fori_loop(0, cycle_size, backward_turn, second_state)
    query_acc = second_out[4]
    key_acc = second_out[5]
    value_acc = second_out[6]
    queries_grad = (query_acc * scale).astype(jnp.bfloat16)[None]
    kv_grad = jnp.concatenate([key_acc * scale, value_acc], 1).astype(jnp.bfloat16)
    enc_grad = lax.dot_general(
        kv_grad, w_full, (((1,), (1,)), ((), ())), preferred_element_type=jnp.float32
    )
    gated_grad = enc_grad * silu_slope(gated)
    gain_term = jnp.sum(gated_grad * conv_out, axis=0)
    conv_grad = gated_grad * conv_gain
    tap_terms = jnp.stack(
        [
            jnp.sum(conv_grad * padded[tap_idx : tap_idx + length].astype(jnp.float32), axis=0)
            for tap_idx in range(tap_count)
        ]
    )
    padded_grad = padded_2(conv_grad[None], (("ctx", 1),), rim_width)[0]
    back_conv = jnp.zeros((length, model_width), jnp.float32)
    for tap_idx in range(tap_count):
        offset = 2 * rim_width - tap_idx
        back_conv = back_conv + conv_taps[tap_idx] * padded_grad[offset : offset + length]
    frames_grad = (enc_grad + back_conv).astype(jnp.bfloat16)[None]
    taps_grad, gain_grad = lax.psum((tap_terms, gain_term), ("dp", "ctx"))
    data_part = lax.psum_scatter(
        lax.dot_general(
            encoded, kv_grad, (((0,), (0,)), ((), ())), preferred_element_type=jnp.float32
        ),
        "dp",
        scatter_dimension=0,
        tiled=True,
    )
    w_kv_grad = lax.psum(data_part, "ctx")
    return (frames_grad, taps_grad, gain_grad, w_kv_grad, queries_grad)


def solution(mesh):
    placed = (
        P("dp", "ctx", None),
        P(),
        P(),
        P("dp", None),
        P("dp", "ctx", None),
        P("dp", "ctx", None),
        P("dp"),
        P("dp"),
    )
    return jax.shard_map(
        per_device,
        mesh=mesh,
        in_specs=placed,
        out_specs=(P("dp", "ctx", None), P(), P(), P("dp", None), P("dp", "ctx", None)),
        check_vma=False,
    )
```

profile of v0, /device:TPU:0, one launch (start us, length us, event | category | flops | bytes accessed | tf_op | source)
XLA Modules:
  0.0 496.1 jit_solution(5663490250576671858)
XLA Ops:
  9.6 4.8 collective-permute-start.8
  18.0 1.8 slice_reduce_fusion.30
  22.3 12.4 %fusion.82 = (bf16[512,1280]{1,0:T(8,128)(2,1)}, f32[512,1280]{1,0:T(8,128)}) fusion(bf16[1,512,1280]{2,1,0:T(8,128)(2,1)S(1)} %copy-done.4, f32[1280]{0:T(1024)S(1)} %copy-done.75, bf16[1,527,1280]{2,1,0:T(8,128)(2,1)S(1)} %constant_dynamic-update-slice_fusion, f32[1280]{0:T(1024)S(1)} %get-tuple-element.290, f32[1280]{0:T(1024)S(1)} %get-tuple-element.291, ...), kind=kLoop, calls=%fused_computation.196 | loop fusion | flops 104202240 | bytes 25105920 | tf_op jit(solution)/shard_map/convert_element_type | solution.py:113
  35.0 41.4 %all-gather.2.cloned.1.call-done = bf16[1280,2560]{1,0:T(8,128)(2,1)} async-done(((bf16[80,2560]{1,0:T(8,128)(2,1)}), bf16[1280,2560]{1,0:T(8,128)(2,1)}) %all-gather.2.cloned.1.call-update) | async-done | bytes 6553616 | tf_op jit(solution)/shard_map/all_gather | solution.py:114
  76.4 6.8 %convolution_convert_fusion = bf16[512,2560]{1,0:T(8,128)(2,1)S(1)} fusion(bf16[512,1280]{1,0:T(8,128)(2,1)} %get-tuple-element.335, bf16[1280,2560]{1,0:T(8,128)(2,1)} %all-gather.2.cloned.1.call-done), kind=kOutput, calls=%fused_computation.72 | convolution fusion | flops 3356753920 | bytes 10485760 | tf_op jit(solution)/shard_map/dot_general | solution.py:115
  86.6 2.4 copy.42
  89.6 19.6 %while.38 = (s32[]{:T(128)}, bf16[16,1280]{1,0:T(8,128)(2,1)S(1)}, f32[16,1280]{1,0:T(8,128)S(1)}, f32[16,20]{0,1:T(8,128)}, bf16[512,1280]{0,1:T(8,128)(2,1)}, ...) while((s32[]{:T(128)}, bf16[16,1280]{1,0:T(8,128)(2,1)S(1)}, ...), condition=%wide.region_2.3_spmd.clone, body=%wide.region_0.2_spmd.clone.sunk | while | flops 42620416 | bytes 4643037 | solution.py:153
  97.1 2.3 collective-permute-done.2
  106.9 2.3 collective-permute-done.2
  112.5 56.3 %while.39 = (s32[]{:T(128)}, bf16[16,1280]{1,0:T(8,128)(2,1)}, bf16[16,1280]{1,0:T(8,128)(2,1)}, f32[16,20]{0,1:T(8,128)}, f32[16,20]{0,1:T(8,128)}, /*index=5*/...) while((s32[]{:T(128)}, bf16[16,1280]{1,0:T(8,128)(2,1)}, ...), condition=%wide.region_5.6_spmd.clone, body=%wide.region_4.5_spmd.clone.sunk | while | flops 108647936 | bytes 37869488 | solution.py:185
  121.6 1.7 fusion.292
  128.3 3.1 fusion.294
  131.4 2.1 fusion.295
  133.5 6.1 %bitcast_add_fusion.6 = (f32[512,1280]{0,1:T(8,128)}, f32[512,1280]{0,1:T(8,128)}) fusion(f32[20,512,64]{1,2,0:T(8,128)} %fusion.294, f32[512,1280]{0,1:T(8,128)} %get-tuple-element.528, pred[]{:T(512)S(6)} %compare.3, f32[20,512,64]{1,2,0:T(8,128)} %fusion.295, f32[512,1280]{0,1:T(8,128)} %get-tuple-element.527), kind=kLoop, calls=%fused_computation.11.clone.1 | loop fusion | flops 2621440 | bytes 15728641 | tf_op jit(solution)/shard_map/while/body/eval_jaxpr/add | solution.py:173
  149.5 1.7 fusion.292
  155.2 3.1 fusion.294
  158.4 2.1 fusion.295
  160.5 7.7 %bitcast_add_fusion.6 = (f32[512,1280]{0,1:T(8,128)}, f32[512,1280]{0,1:T(8,128)}) fusion(f32[20,512,64]{1,2,0:T(8,128)} %fusion.294, f32[512,1280]{0,1:T(8,128)} %get-tuple-element.528, pred[]{:T(512)S(6)} %compare.3, f32[20,512,64]{1,2,0:T(8,128)} %fusion.295, f32[512,1280]{0,1:T(8,128)} %get-tuple-element.527), kind=kLoop, calls=%fused_computation.11.clone.1 | loop fusion | flops 2621440 | bytes 15728641 | tf_op jit(solution)/shard_map/while/body/eval_jaxpr/add | solution.py:173
  168.8 2.2 multiply_convert_fusion
  172.6 7.7 %fusion.204 = f32[1280,2560]{1,0:T(8,128)} fusion(bf16[512,1280]{1,0:T(8,128)(2,1)S(1)} %copy-done.10, bf16[512,1280]{0,1:T(8,128)(2,1)S(1)} %convert.38, bf16[512,1280]{0,1:T(8,128)(2,1)S(1)} %multiply_convert_fusion), kind=kOutput, calls=%fused_computation.348 | convolution fusion | flops 3360686080 | bytes 17039360 | tf_op jit(solution)/shard_map/dot_general | solution.py:211
  180.6 7.0 %fusion.205 = f32[512,1280]{1,0:T(8,128)S(1)} fusion(bf16[1280,2560]{1,0:T(8,128)(2,1)} %all-gather.2.cloned.1.call-done, bf16[512,1280]{0,1:T(8,128)(2,1)} %copy-done.11, bf16[512,1280]{0,1:T(8,128)(2,1)S(1)} %multiply_convert_fusion), kind=kOutput, calls=%fused_computation.349 | convolution fusion | flops 3360686080 | bytes 11796480 | tf_op jit(solution)/shard_map/dot_general | solution.py:191
  187.7 6.7 %fusion.81 = (f32[1280]{0:T(1024)S(1)}, f32[1280]{0:T(1024)S(1)}, f32[1280]{0:T(1024)S(1)}, f32[1280]{0:T(1024)S(1)}, f32[1280]{0:T(1024)S(1)}, /*index=5*/f32[1...) fusion(bf16[1,527,1280]{2,1,0:T(8,128)(2,1)S(1)} %constant_dyna, ...), kind=kLoop, calls=%fused_computation.195 | loop fusion | flops 37335040 | bytes 27612160 | tf_op jit(solution)/shard_map/reduce_sum | solution.py:199
  194.6 2.6 fusion.52
  197.6 3.3 fusion.61
  202.3 4.6 collective-permute-start.11
  206.9 2.7 stack.127
  210.3 44.2 %psum.22 = f32[1280]{0:T(1024)} all-reduce(f32[1280]{0:T(1024)S(1)} %get-tuple-element.341), channel_id=1, replica_groups=mesh['dp'=16,'ctx'=2] {'dp','ctx'}, use_global_device_ids=true, to_apply=%region_39.40 | all-reduce | flops 1280 | bytes 10240 | tf_op jit(solution)/shard_map/psum | solution.py:209
  254.5 64.0 %reduce-scatter.2.cloned.1.call-done = f32[80,2560]{1,0:T(8,128)} async-done(((f32[1280,2560]{1,0:T(8,128)}), f32[80,2560]{1,0:T(8,128)}) %reduce-scatter.2.cloned.1.call-update) | async-done | bytes 819216 | tf_op jit(solution)/shard_map/reduce_scatter | solution.py:210
  318.8 43.9 %fusion.235 = bf16[1,512,1280]{2,1,0:T(8,128)(2,1)} fusion(f32[512,1280]{1,0:T(8,128)} %copy-done.6, f32[1,512,1280]{2,1,0:T(8,128)} %bitcast.634, f32[1,15,1280]{2,1,0:T(8,128)S(1)} %collective-permute-done.11, f32[1280]{0:T(1024)S(1)} %copy-done.33, f32[1280]{0:T(1024)S(1)} %copy-done.35, f32[1280]{0:T(1024)S(1)} %copy-done.39, f32[1280]{0:T(1024)S(1)} %copy-done.41, ...), kind=kLoop, calls=%fused_computation.396 | loop fusion | flops 60948480 | bytes 9487360 | tf_op jit(solution)/shard_map/broadcast_in_dim | solution.py:208
  362.7 83.9 %all-reduce.3.cloned.1.call-done = f32[31,1280]{1,0:T(8,128)} async-done(((f32[31,1280]{1,0:T(8,128)}), f32[31,1280]{1,0:T(8,128)}) %all-reduce.3.cloned.1.call-update) | async-done | bytes 158736 | tf_op jit(solution)/shard_map/psum | solution.py:209
  446.5 39.3 %all-reduce.5.cloned.1.call-done = f32[80,2560]{1,0:T(8,128)} async-done(((f32[80,2560]{1,0:T(8,128)}), f32[80,2560]{1,0:T(8,128)}) %all-reduce.5.cloned.1.call-update) | async-done | bytes 819216 | tf_op jit(solution)/shard_map/psum | solution.py:218
  487.5 2.1 copy.118
  (302 shorter events, 63.7 us)
Async XLA Ops:
  7.2 69.2 %all-gather.2.cloned.1.call-start = ((), (), s32[]{:S(2)}) async-start(), calls=%async_computation.1 | async-start | bytes 6963200 | tf_op jit(solution)/shard_map/all_gather | solution.py:114
  8.7 309.7 %reduce-scatter.2.cloned.1.call-start = ((), (), s32[]{:S(2)}) async-start(), calls=%async_computation.3 | async-start | bytes 13926400 | tf_op jit(solution)/shard_map/reduce_scatter | solution.py:210
  9.6 12.7 %collective-permute-start.8 = (bf16[1,15,1280]{2,1,0:T(8,128)(2,1)S(1)}, bf16[1,15,1280]{2,1,0:T(8,128)(2,1)S(1)}, u32[]{:S(2)}, u32[]{:S(2)}) collective-permute-start(bf16[1,15,1280]{2,1,0:T(8,128)(2,1)S(1)} %get-tuple-element.346), channel_id=1, source_target_pairs={{0,1},{2,3},{4,5},{6,7},{8,9},{10,11},{12,13},{14,15},{16,17},{18,... | collective-permute-start | bytes 115208 | tf_op jit(solution)/shard_map/ppermute | solution.py:14
  14.5 7.8 %collective-permute-start.9 = (bf16[1,15,1280]{2,1,0:T(8,128)(2,1)S(1)}, bf16[1,15,1280]{2,1,0:T(8,128)(2,1)S(1)}, u32[]{:S(2)}, u32[]{:S(2)}) collective-permute-start(bf16[1,15,1280]{2,1,0:T(8,128)(2,1)S(1)} %get-tuple-element.347), channel_id=1, source_target_pairs={{1,0},{3,2},{5,4},{7,6},{9,8},{11,10},{13,12},{15,14},{17,16},{19,... | collective-permute-start | bytes 115208 | tf_op jit(solution)/shard_map/ppermute | solution.py:17
  89.7 9.8 %collective-permute-start = (bf16[16,1280]{1,0:T(8,128)(2,1)S(1)}, bf16[16,1280]{1,0:T(8,128)(2,1)S(1)}, u32[]{:S(2)}, u32[]{:S(2)}) collective-permute-start(bf16[16,1280]{1,0:T(8,128)(2,1)S(1)} %copy.80), channel_id=1, source_target_pairs={{0,1},{1,0},{2,3},{3,2},{4,5},{5,4},{6,7},{7,6},{8,9},{9,8},{10,11... | collective-permute-start | bytes 122888 | tf_op jit(solution)/shard_map/while/body/eval_jaxpr/ppermute | solution.py:25
  94.3 5.1 %collective-permute-start.1 = (f32[16,1280]{1,0:T(8,128)S(1)}, f32[16,1280]{1,0:T(8,128)S(1)}, u32[]{:S(2)}, u32[]{:S(2)}) collective-permute-start(f32[16,1280]{1,0:T(8,128)S(1)} %add.1592), channel_id=1, source_target_pairs={{0,1},{1,0},{2,3},{3,2},{4,5},{5,4},{6,7},{7,6},{8,9},{9,8},{10,11... | collective-permute-start | bytes 245768 | tf_op jit(solution)/shard_map/while/body/eval_jaxpr/ppermute | solution.py:25
  95.7 3.8 collective-permute-start.2
  99.5 9.8 %collective-permute-start = (bf16[16,1280]{1,0:T(8,128)(2,1)S(1)}, bf16[16,1280]{1,0:T(8,128)(2,1)S(1)}, u32[]{:S(2)}, u32[]{:S(2)}) collective-permute-start(bf16[16,1280]{1,0:T(8,128)(2,1)S(1)} %copy.80), channel_id=1, source_target_pairs={{0,1},{1,0},{2,3},{3,2},{4,5},{5,4},{6,7},{7,6},{8,9},{9,8},{10,11... | collective-permute-start | bytes 122888 | tf_op jit(solution)/shard_map/while/body/eval_jaxpr/ppermute | solution.py:25
  104.1 5.1 %collective-permute-start.1 = (f32[16,1280]{1,0:T(8,128)S(1)}, f32[16,1280]{1,0:T(8,128)S(1)}, u32[]{:S(2)}, u32[]{:S(2)}) collective-permute-start(f32[16,1280]{1,0:T(8,128)S(1)} %add.1592), channel_id=1, source_target_pairs={{0,1},{1,0},{2,3},{3,2},{4,5},{5,4},{6,7},{7,6},{8,9},{9,8},{10,11... | collective-permute-start | bytes 245768 | tf_op jit(solution)/shard_map/while/body/eval_jaxpr/ppermute | solution.py:25
  105.5 3.8 collective-permute-start.2
  113.8 25.9 %collective-permute-start.5 = (f32[16,20]{0,1:T(8,128)}, f32[16,20]{0,1:T(8,128)}, u32[]{:S(2)}, u32[]{:S(2)}) collective-permute-start(f32[16,20]{0,1:T(8,128)} %copy.98), channel_id=1, source_target_pairs={{0,1},{1,0},{2,3},{3,2},{4,5},{5,4},{6,7},{7,6},{8,9},{9,8},{10,11... | collective-permute-start | bytes 3848 | tf_op jit(solution)/shard_map/while/body/eval_jaxpr/ppermute | solution.py:25
  116.6 23.1 %collective-permute-start.6 = (f32[16,20]{0,1:T(8,128)}, f32[16,20]{0,1:T(8,128)}, u32[]{:S(2)}, u32[]{:S(2)}) collective-permute-start(f32[16,20]{0,1:T(8,128)} %copy.99), channel_id=1, source_target_pairs={{0,1},{1,0},{2,3},{3,2},{4,5},{5,4},{6,7},{7,6},{8,9},{9,8},{10,11... | collective-permute-start | bytes 3848 | tf_op jit(solution)/shard_map/while/body/eval_jaxpr/ppermute | solution.py:25
  117.9 21.8 %collective-permute-start.3 = (bf16[16,1280]{1,0:T(8,128)(2,1)S(1)}, bf16[16,1280]{1,0:T(8,128)(2,1)}, u32[]{:S(2)}, u32[]{:S(2)}) collective-permute-start(bf16[16,1280]{1,0:T(8,128)(2,1)S(1)} %copy.96), channel_id=1, source_target_pairs={{0,1},{1,0},{2,3},{3,2},{4,5},{5,4},{6,7},{7,6},{8,9},{9,8},{10,11... | collective-permute-start | bytes 122888 | tf_op jit(solution)/shard_map/while/body/eval_jaxpr/ppermute | solution.py:25
  120.2 19.5 %collective-permute-start.4 = (bf16[16,1280]{1,0:T(8,128)(2,1)S(1)}, bf16[16,1280]{1,0:T(8,128)(2,1)}, u32[]{:S(2)}, u32[]{:S(2)}) collective-permute-start(bf16[16,1280]{1,0:T(8,128)(2,1)S(1)} %copy.97), channel_id=1, source_target_pairs={{0,1},{1,0},{2,3},{3,2},{4,5},{5,4},{6,7},{7,6},{8,9},{9,8},{10,11... | collective-permute-start | bytes 122888 | tf_op jit(solution)/shard_map/while/body/eval_jaxpr/ppermute | solution.py:25
  126.7 13.0 %collective-permute-start.7 = (f32[16,1280]{1,0:T(8,128)S(1)}, f32[16,1280]{1,0:T(8,128)S(1)}, u32[]{:S(2)}, u32[]{:S(2)}) collective-permute-start(f32[16,1280]{1,0:T(8,128)S(1)} %add.1597), channel_id=1, source_target_pairs={{0,1},{1,0},{2,3},{3,2},{4,5},{5,4},{6,7},{7,6},{8,9},{9,8},{10,11... | collective-permute-start | bytes 245768 | tf_op jit(solution)/shard_map/while/body/eval_jaxpr/ppermute | solution.py:25
  141.7 26.5 %collective-permute-start.5 = (f32[16,20]{0,1:T(8,128)}, f32[16,20]{0,1:T(8,128)}, u32[]{:S(2)}, u32[]{:S(2)}) collective-permute-start(f32[16,20]{0,1:T(8,128)} %copy.98), channel_id=1, source_target_pairs={{0,1},{1,0},{2,3},{3,2},{4,5},{5,4},{6,7},{7,6},{8,9},{9,8},{10,11... | collective-permute-start | bytes 3848 | tf_op jit(solution)/shard_map/while/body/eval_jaxpr/ppermute | solution.py:25
  143.5 24.6 %collective-permute-start.6 = (f32[16,20]{0,1:T(8,128)}, f32[16,20]{0,1:T(8,128)}, u32[]{:S(2)}, u32[]{:S(2)}) collective-permute-start(f32[16,20]{0,1:T(8,128)} %copy.99), channel_id=1, source_target_pairs={{0,1},{1,0},{2,3},{3,2},{4,5},{5,4},{6,7},{7,6},{8,9},{9,8},{10,11... | collective-permute-start | bytes 3848 | tf_op jit(solution)/shard_map/while/body/eval_jaxpr/ppermute | solution.py:25
  145.8 22.4 %collective-permute-start.3 = (bf16[16,1280]{1,0:T(8,128)(2,1)S(1)}, bf16[16,1280]{1,0:T(8,128)(2,1)}, u32[]{:S(2)}, u32[]{:S(2)}) collective-permute-start(bf16[16,1280]{1,0:T(8,128)(2,1)S(1)} %copy.96), channel_id=1, source_target_pairs={{0,1},{1,0},{2,3},{3,2},{4,5},{5,4},{6,7},{7,6},{8,9},{9,8},{10,11... | collective-permute-start | bytes 122888 | tf_op jit(solution)/shard_map/while/body/eval_jaxpr/ppermute | solution.py:25
  147.1 21.1 %collective-permute-start.4 = (bf16[16,1280]{1,0:T(8,128)(2,1)S(1)}, bf16[16,1280]{1,0:T(8,128)(2,1)}, u32[]{:S(2)}, u32[]{:S(2)}) collective-permute-start(bf16[16,1280]{1,0:T(8,128)(2,1)S(1)} %copy.97), channel_id=1, source_target_pairs={{0,1},{1,0},{2,3},{3,2},{4,5},{5,4},{6,7},{7,6},{8,9},{9,8},{10,11... | collective-permute-start | bytes 122888 | tf_op jit(solution)/shard_map/while/body/eval_jaxpr/ppermute | solution.py:25
  154.6 13.6 %collective-permute-start.7 = (f32[16,1280]{1,0:T(8,128)S(1)}, f32[16,1280]{1,0:T(8,128)S(1)}, u32[]{:S(2)}, u32[]{:S(2)}) collective-permute-start(f32[16,1280]{1,0:T(8,128)S(1)} %add.1597), channel_id=1, source_target_pairs={{0,1},{1,0},{2,3},{3,2},{4,5},{5,4},{6,7},{7,6},{8,9},{9,8},{10,11... | collective-permute-start | bytes 245768 | tf_op jit(solution)/shard_map/while/body/eval_jaxpr/ppermute | solution.py:25
  180.4 266.2 %all-reduce.3.cloned.1.call-start = ((), (), s32[]{:S(2)}) async-start(), calls=%async_computation.2 | async-start | bytes 327680 | tf_op jit(solution)/shard_map/psum | solution.py:209
  197.3 121.2 %copy-start.15 = (f32[1280]{0:T(1024)S(1)}, f32[1280]{0:T(1024)}, u32[]{:S(2)}) copy-start(f32[1280]{0:T(1024)} %copy-done.14) | copy-start | bytes 15364
  197.3 121.2 %copy-start.17 = (f32[1280]{0:T(1024)S(1)}, f32[1280]{0:T(1024)}, u32[]{:S(2)}) copy-start(f32[1280]{0:T(1024)} %copy-done.16) | copy-start | bytes 15364
  197.3 121.2 %copy-start.19 = (f32[1280]{0:T(1024)S(1)}, f32[1280]{0:T(1024)}, u32[]{:S(2)}) copy-start(f32[1280]{0:T(1024)} %copy-done.18) | copy-start | bytes 15364
  197.3 121.2 %copy-start.21 = (f32[1280]{0:T(1024)S(1)}, f32[1280]{0:T(1024)}, u32[]{:S(2)}) copy-start(f32[1280]{0:T(1024)} %copy-done.20) | copy-start | bytes 15364
  197.3 121.2 %copy-start.23 = (f32[1280]{0:T(1024)S(1)}, f32[1280]{0:T(1024)}, u32[]{:S(2)}) copy-start(f32[1280]{0:T(1024)} %copy-done.22) | copy-start | bytes 15364
  197.3 121.2 %copy-start.25 = (f32[1280]{0:T(1024)S(1)}, f32[1280]{0:T(1024)}, u32[]{:S(2)}) copy-start(f32[1280]{0:T(1024)} %copy-done.24) | copy-start | bytes 15364
  197.3 121.2 %copy-start.27 = (f32[1280]{0:T(1024)S(1)}, f32[1280]{0:T(1024)}, u32[]{:S(2)}) copy-start(f32[1280]{0:T(1024)} %copy-done.26) | copy-start | bytes 15364
  197.4 121.2 %copy-start.29 = (f32[1280]{0:T(1024)S(1)}, f32[1280]{0:T(1024)}, u32[]{:S(2)}) copy-start(f32[1280]{0:T(1024)} %copy-done.28) | copy-start | bytes 15364
  201.0 117.5 %collective-permute-start.10 = (f32[1,15,1280]{2,1,0:T(8,128)S(1)}, f32[1,15,1280]{2,1,0:T(8,128)S(1)}, u32[]{:S(2)}, u32[]{:S(2)}) collective-permute-start(f32[1,15,1280]{2,1,0:T(8,128)S(1)} %get-tuple-element.342), channel_id=1, source_target_pairs={{1,0},{3,2},{5,4},{7,6},{9,8},{11,10},{13,12},{15,14},{17,16},{19,... | collective-permute-start | bytes 230408 | tf_op jit(solution)/shard_map/ppermute | solution.py:17
  202.3 116.2 %collective-permute-start.11 = (f32[1,15,1280]{2,1,0:T(8,128)S(1)}, f32[1,15,1280]{2,1,0:T(8,128)S(1)}, u32[]{:S(2)}, u32[]{:S(2)}) collective-permute-start(f32[1,15,1280]{2,1,0:T(8,128)S(1)} %get-tuple-element.343), channel_id=1, source_target_pairs={{0,1},{2,3},{4,5},{6,7},{8,9},{10,11},{12,13},{14,15},{16,17},{18,... | collective-permute-start | bytes 230408 | tf_op jit(solution)/shard_map/ppermute | solution.py:14
  209.6 276.3 %all-reduce.5.cloned.1.call-start = ((), (), s32[]{:S(2)}) async-start(), calls=%async_computation.4 | async-start | bytes 1638400 | tf_op jit(solution)/shard_map/psum | solution.py:218
  (72 other events, 3271.5 us)
Sparse Core Ops, SparseCore 0:
  10.3 66.0 all-gather.1
  180.5 137.9 reduce-scatter.1
  325.5 120.9 all-reduce.2
  448.8 37.0 all-reduce.4
where the time goes:
time: 498 us; the launch traced here: 496 us
  waiting for transfers between devices  233 us (47%)
  other arithmetic  92.3 us (19%)
  blocking collectives  44.2 us (9%)
  matrix products  42.7 us (9%)
  local copies, waits for them, and re-layouts  37.5 us (8%)
  starting transfers between devices  29.8 us (6%)
  between operations  16 us (3%)
    psum x1, waiting for transfers between devices, per_device(): taps_grad, gain_grad = lax.psum((tap_terms, gain_term), ('dp', 'ctx'))  83.9 us
    reduce_scatter x1, waiting for transfers between devices, per_device(): lax.psum_scatter(lax.dot_general(encoded, kv_grad, (((0,), (0,)), ((), ()...  64 us
    psum x1, blocking collectives, per_device(): taps_grad, gain_grad = lax.psum((tap_terms, gain_term), ('dp', 'ctx'))  44.2 us
    broadcast_in_dim x1, other arithmetic, per_device(): frames_grad = (enc_grad + back_conv).astype(jnp.bfloat16)[None]  43.9 us
    all_gather x1, waiting for transfers between devices, per_device(): w_full = lax.all_gather(w_kv, 'dp', axis=0, tiled=True)  41.4 us
    psum x1, waiting for transfers between devices, per_device(): w_kv_grad = lax.psum(data_part, 'ctx')  39.3 us
    ppermute x16, starting transfers between devices, shifted(): return lax.ppermute(value, axis, pairs)  17.5 us
    unnamed x156, local copies, waits for them, and re-layouts  13.9 us
  transfers between devices with their start and end apart: 24, of which 6 were waited for; matrix products, arithmetic and copies ran while one was open for 27% of the time, Pallas kernels for 0%

commit v1 on v0

v1 whole, which is shorter than its diff:
```python
import functools

import jax
import jax.numpy as jnp
from jax import lax
from jax.experimental import pallas as pl
from jax.experimental.pallas import tpu as pltpu
from jax.sharding import PartitionSpec as P

HEADS = 20
PACK = 4
LANES = 128
VMEM_BYTES = 48 * 1024 * 1024
F32 = jnp.float32
BF16 = jnp.bfloat16


def shifted(value, axis, steps):
    count = lax.axis_size(axis)
    pairs = [(source, (source + steps) % count) for source in range(count)]
    return lax.ppermute(value, axis, pairs)


def rims(block, width):
    count = lax.axis_size("ctx")
    forward = [(i, i + 1) for i in range(count - 1)]
    backward = [(i + 1, i) for i in range(count - 1)]
    low = lax.ppermute(block[block.shape[0] - width :], "ctx", forward)
    high = lax.ppermute(block[:width], "ctx", backward)
    return low, high


def gather_tokens(block):
    parts = [block]
    for step in range(1, lax.axis_size("ctx")):
        parts.append(shifted(block, "ctx", step))
    return jnp.concatenate(parts, axis=0)


def sum_ctx(value):
    total = value
    for step in range(1, lax.axis_size("ctx")):
        total = total + shifted(value, "ctx", step)
    return total


def sum_all(value):
    for axis in ("dp", "ctx"):
        count = lax.axis_size(axis)
        if count & (count - 1):
            value = lax.psum(value, axis)
            continue
        step = 1
        while step < count:
            value = value + lax.ppermute(value, axis, [(i, i ^ step) for i in range(count)])
            step *= 2
    return value


def conv_time(padded, conv_taps, length):
    total = jnp.zeros((length, padded.shape[1]), F32)
    for tap_idx in range(conv_taps.shape[0]):
        total = total + conv_taps[tap_idx] * padded[tap_idx : tap_idx + length].astype(F32)
    return total


def packed(block, scale):
    tokens, width = block.shape
    groups = HEADS // PACK
    cols = width // groups
    head_dim = cols // PACK
    rows = block.reshape(tokens, groups, cols).transpose(1, 0, 2)[:, None]
    own = (jnp.arange(cols)[None] // head_dim == jnp.arange(PACK)[:, None]).astype(F32) * scale
    return (rows.astype(F32) * own[None, :, None, :]).astype(BF16).reshape(groups, PACK * tokens, cols)


def score_kernel(limit_ref, kv_ref, q_ref, g_ref, e_ref, d_ref, s_ref):
    groups, lanes, cols = q_ref.shape
    length = kv_ref.shape[0]
    width = groups * cols
    live = lax.broadcasted_iota(jnp.int32, (length, lanes), 0) < limit_ref[0]
    dims = (((1,), (1,)), ((), ()))
    s_ref[...] = jnp.zeros_like(s_ref)
    for j in range(groups):
        keys = kv_ref[:, j * cols : (j + 1) * cols]
        values = kv_ref[:, width + j * cols : width + (j + 1) * cols]
        scores = lax.dot_general(keys, q_ref[j], dims, preferred_element_type=F32)
        exps = jnp.where(live, jnp.exp(scores), 0.0)
        dprob = lax.dot_general(values, g_ref[j], dims, preferred_element_type=F32)
        e_ref[:, j * lanes : (j + 1) * lanes] = exps
        d_ref[:, j * lanes : (j + 1) * lanes] = dprob
        s_ref[j : j + 1] = jnp.sum(exps, axis=0, keepdims=True)
        s_ref[8 + j : 9 + j] = jnp.sum(exps.astype(BF16).astype(F32) * dprob, axis=0, keepdims=True)


def grad_kernel(e_ref, d_ref, s_ref, kv_ref, q_ref, g_ref, kvg_ref, qg_ref):
    groups, lanes, cols = q_ref.shape
    width = groups * cols
    tokens = lanes // PACK
    head_dim = cols // PACK
    head_of = lax.broadcasted_iota(jnp.int32, (tokens, cols), 1) // head_dim
    for j in range(groups):
        inverse = 1.0 / s_ref[j : j + 1]
        delta = s_ref[8 + j : 9 + j] * inverse
        prob = e_ref[:, j * lanes : (j + 1) * lanes] * inverse
        dscore = (prob * (d_ref[:, j * lanes : (j + 1) * lanes] - delta)).astype(BF16)
        kvg_ref[:, j * cols : (j + 1) * cols] = jnp.dot(
            dscore, q_ref[j], preferred_element_type=F32
        ).astype(BF16)
        kvg_ref[:, width + j * cols : width + (j + 1) * cols] = jnp.dot(
            prob.astype(BF16), g_ref[j], preferred_element_type=F32
        ).astype(BF16)
        full = lax.dot_general(
            dscore,
            kv_ref[:, j * cols : (j + 1) * cols],
            (((0,), (0,)), ((), ())),
            preferred_element_type=F32,
        )
        total = jnp.zeros((tokens, cols), F32)
        for h in range(PACK):
            total = total + jnp.where(head_of == h, full[h * tokens : (h + 1) * tokens], 0.0)
        qg_ref[:, j * cols : (j + 1) * cols] = total


def taps_kernel(tap_count, g_ref, x_ref, t_ref):
    length = g_ref.shape[0]

    def step(i, sums):
        base = pl.multiple_of(i * 8, 8)
        grad = g_ref[pl.ds(base, 8), :]
        return tuple(sums[k] + grad * x_ref[pl.ds(base + k, 8), :] for k in range(tap_count))

    zero = jnp.zeros((8, g_ref.shape[1]), F32)
    sums = lax.fori_loop(0, length // 8, step, (zero,) * tap_count)
    t_ref[...] = jnp.zeros_like(t_ref)
    for k in range(tap_count):
        t_ref[k : k + 1, :] = jnp.sum(sums[k], axis=0, keepdims=True)


def back_kernel(tap_count, taps_ref, g_ref, e_ref, o_ref):
    rows = 64

    def step(i, carry):
        base = pl.multiple_of(i * rows, rows)
        total = e_ref[pl.ds(base, rows), :]
        for k in range(tap_count):
            total = total + taps_ref[k : k + 1, :] * g_ref[pl.ds(base + tap_count - 1 - k, rows), :]
        o_ref[pl.ds(base, rows), :] = total.astype(BF16)
        return carry

    lax.fori_loop(0, e_ref.shape[0] // rows, step, 0)


def whole_spec():
    return pl.BlockSpec(memory_space=pltpu.VMEM)


def column_spec(rows):
    return pl.BlockSpec((rows, LANES), lambda j: (0, j))


def per_device(frames, conv_taps, conv_gain, w_kv, queries, out_grad, frame_len, token_len):
    cycle_pos = lax.axis_index("ctx")
    length = frames.shape[1]
    width = frames.shape[2]
    tokens = queries.shape[1]
    tap_count = conv_taps.shape[0]
    rim = tap_count // 2
    scale = (width // HEADS) ** (-0.5)
    params = pltpu.CompilerParams(vmem_limit_bytes=VMEM_BYTES)

    w_full = lax.all_gather(w_kv, "dp", axis=0, tiled=True)
    block = frames[0]
    low, high = rims(block, rim)
    tail = -(length + 2 * rim) % 16
    padded = jnp.concatenate([low, block, high, jnp.zeros((tail, width), BF16)], axis=0).astype(F32)
    conv_out = conv_time(padded, conv_taps, length)
    gated = conv_gain * conv_out
    sigma = jax.nn.sigmoid(gated)
    encoded = (block.astype(F32) + gated * sigma).astype(BF16)
    slope = sigma * (1.0 + gated * (1.0 - sigma))

    token_pos = cycle_pos * tokens + jnp.arange(tokens)
    grad_block = out_grad[0] * (token_pos < token_len[0]).astype(BF16)[:, None]
    q_pack = packed(gather_tokens(queries[0]), scale)
    g_pack = packed(gather_tokens(grad_block), 1.0)
    groups, lanes, _ = q_pack.shape
    all_tokens = lanes // PACK
    limit = (frame_len - cycle_pos * length).astype(jnp.int32)

    key_values = jnp.dot(encoded, w_full, preferred_element_type=F32).astype(BF16)
    exps, dprob, stats = pl.pallas_call(
        score_kernel,
        out_shape=(
            jax.ShapeDtypeStruct((length, groups * lanes), F32),
            jax.ShapeDtypeStruct((length, groups * lanes), F32),
            jax.ShapeDtypeStruct((16, lanes), F32),
        ),
        in_specs=[pl.BlockSpec(memory_space=pltpu.SMEM)] + [whole_spec()] * 3,
        out_specs=(whole_spec(),) * 3,
        compiler_params=params,
    )(limit, key_values, q_pack, g_pack)
    count = lax.axis_size("ctx")
    parts = stats.reshape(16, PACK, count, tokens)
    total_parts = parts
    for step in range(1, count):
        total_parts = total_parts + jnp.roll(shifted(parts, "ctx", step), step, axis=2)
    stats = total_parts.reshape(16, lanes)
    kv_grad, q_part = pl.pallas_call(
        grad_kernel,
        out_shape=(
            jax.ShapeDtypeStruct((length, 2 * width), BF16),
            jax.ShapeDtypeStruct((all_tokens, width), F32),
        ),
        in_specs=[whole_spec()] * 6,
        out_specs=(whole_spec(),) * 2,
        compiler_params=params,
    )(exps, dprob, stats, key_values, q_pack, g_pack)

    w_part = lax.dot_general(
        encoded, kv_grad, (((0,), (0,)), ((), ())), preferred_element_type=F32
    ).astype(BF16)
    w_rows = lax.psum_scatter(w_part, "dp", scatter_dimension=0, tiled=True)

    q_parts = q_part.reshape(count, tokens, width)
    q_sum = q_parts[0]
    for step in range(1, count):
        q_sum = q_sum + shifted(q_parts[step], "ctx", -step)
    queries_grad = (q_sum * scale).astype(BF16)[None]

    enc_grad = lax.dot_general(
        kv_grad, w_full, (((1,), (1,)), ((), ())), preferred_element_type=F32
    )
    gated_grad = enc_grad * slope
    grad_low, grad_high = rims(gated_grad, rim)
    tap_rows = -(-tap_count // 8) * 8
    tap_sums = pl.pallas_call(
        functools.partial(taps_kernel, tap_count),
        grid=(width // LANES,),
        out_shape=jax.ShapeDtypeStruct((tap_rows, width), F32),
        in_specs=[column_spec(length), column_spec(padded.shape[0])],
        out_specs=column_spec(tap_rows),
        compiler_params=params,
    )(gated_grad, padded)
    tap_sums = sum_all(tap_sums)[:tap_count]
    taps_grad = tap_sums * conv_gain
    gain_grad = jnp.sum(tap_sums * conv_taps, axis=0)

    padded_grad = jnp.concatenate(
        [grad_low, gated_grad, grad_high, jnp.zeros((tail, width), F32)], axis=0
    )
    scaled_taps = jnp.concatenate(
        [conv_taps * conv_gain, jnp.zeros((tap_rows - tap_count, width), F32)], axis=0
    )
    frames_grad = pl.pallas_call(
        functools.partial(back_kernel, tap_count),
        grid=(width // LANES,),
        out_shape=jax.ShapeDtypeStruct((length, width), BF16),
        in_specs=[column_spec(tap_rows), column_spec(padded_grad.shape[0]), column_spec(length)],
        out_specs=column_spec(length),
        compiler_params=params,
    )(scaled_taps, padded_grad, enc_grad)[None]

    if count == 2:
        w_kv_grad = w_rows.astype(F32) + shifted(w_rows, "ctx", 1).astype(F32)
    else:
        w_kv_grad = lax.psum(w_rows.astype(F32), "ctx")
    return (frames_grad, taps_grad, gain_grad, w_kv_grad, queries_grad)


def solution(mesh):
    placed = (
        P("dp", "ctx", None),
        P(),
        P(),
        P("dp", None),
        P("dp", "ctx", None),
        P("dp", "ctx", None),
        P("dp"),
        P("dp"),
    )
    return jax.shard_map(
        per_device,
        mesh=mesh,
        in_specs=placed,
        out_specs=(P("dp", "ctx", None), P(), P(), P("dp", None), P("dp", "ctx", None)),
        check_vma=False,
    )
```

time: 498 us -> 219 us (0.44)
  waiting for transfers between devices: 233 us -> 98.8 us
  other arithmetic: 92.3 us -> 18 us
  blocking collectives: 44.2 us -> 0 us
  Pallas kernels: 0 us -> 24.9 us
  local copies, waits for them, and re-layouts: 37.5 us -> 17.1 us
  matrix products: 42.7 us -> 23.2 us
  starting transfers between devices: 29.8 us -> 20.5 us
    psum x2 -> x0, waiting for transfers between devices: 123 us -> none  [the longest x1 83.9 us: per_device(): taps_grad, gain_grad = lax.psum((tap_terms, gain_term), ('dp', 'ctx'))]
    psum x1 -> x0, blocking collectives: 44.2 us -> none  [per_device(): taps_grad, gain_grad = lax.psum((tap_terms, gain_term), ('dp', 'ctx'))]
    broadcast_in_dim x2 -> x1, other arithmetic: 44.5 us -> 0.63 us  [per_device(): queries_grad = (q_sum * scale).astype(BF16)[None]]
    reduce_scatter x1, waiting for transfers between devices: 64 us -> 22.7 us  [per_device(): w_rows = lax.psum_scatter(w_part, 'dp', scatter_dimension=0, tiled=True)]
    ppermute x4 -> x9, waiting for transfers between devices: 0.01 us -> 34.2 us  [the longest x5 34.2 us: sum_all(): lax.ppermute(value, axis, [(i, i ^ step) for i in range(count)])]
    pallas_call x0 -> x4, Pallas kernels: none -> 24.9 us  [the longest x1 13.7 us: per_device(): pl.pallas_call(functools.partial(taps_kernel, tap_count), grid=(width //...]
    dot_general x15 -> x1, matrix products: 27.9 us -> 7.66 us  [per_device(): jnp.dot(encoded, w_full, preferred_element_type=F32).astype(BF16)]
    add x8 -> x6, other arithmetic: 17 us -> 1.07 us  [the longest x1 0.99 us: per_device(): w_kv_grad = w_rows.astype(F32) + shifted(w_rows, 'ctx', 1).astype(F32)]
  transfers between devices with their start and end apart: 24 -> 16, of which waited for: 6 -> 7; matrix products, arithmetic and copies ran while one was open for 27% -> 15% of each run, Pallas kernels for 0% -> 10%
where the time goes in v1:
time: 219 us; the launch traced here: 218 us
  waiting for transfers between devices  98.8 us (45%)
  Pallas kernels  24.9 us (11%)
  matrix products  23.2 us (11%)
  starting transfers between devices  20.5 us (9%)
  other arithmetic  18 us (8%)
  local copies, waits for them, and re-layouts  17.1 us (8%)
  between operations  15.6 us (7%)
    all_gather x1, waiting for transfers between devices, per_device(): w_full = lax.all_gather(w_kv, 'dp', axis=0, tiled=True)  38.4 us
    ppermute x5, waiting for transfers between devices, sum_all(): lax.ppermute(value, axis, [(i, i ^ step) for i in range(count)])  34.2 us
    reduce_scatter x1, waiting for transfers between devices, per_device(): w_rows = lax.psum_scatter(w_part, 'dp', scatter_dimension=0, tiled=True)  22.7 us
    pallas_call x1, Pallas kernels, per_device(): pl.pallas_call(functools.partial(taps_kernel, tap_count), grid=(width //...  13.7 us
    mul x1, other arithmetic, per_device(): gated = conv_gain * conv_out  10.9 us
    unnamed x28, local copies, waits for them, and re-layouts  10.2 us
    dot_general x1, matrix products, per_device(): lax.dot_general(kv_grad, w_full, (((1,), (1,)), ((), ())), preferred_elem...  9.84 us
    ppermute x2, starting transfers between devices, rims(): low = lax.ppermute(block[block.shape[0] - width:], 'ctx', forward)  9.4 us
  transfers between devices with their start and end apart: 16, of which 7 were waited for; matrix products, arithmetic and copies ran while one was open for 15% of the time, Pallas kernels for 10%

profile of v1, /device:TPU:0, one launch (start us, length us, event | category | flops | bytes accessed | tf_op | source)
XLA Modules:
  0.0 218.1 jit_solution(14253231552529648345)
XLA Ops:
  8.8 1.3 collective-permute-start.1
  10.1 4.8 %collective-permute-start = (bf16[15,1280]{1,0:T(8,128)(2,1)S(1)}, bf16[15,1280]{1,0:T(8,128)(2,1)S(1)}, u32[]{:S(2)}, u32[]{:S(2)}) collective-permute-start(bf16[15,1280]{1,0:T(8,128)(2,1)S(1)} %get-tuple-element.48), channel_id=1, source_target_pairs={{0,1},{2,3},{4,5},{6,7},{8,9},{10,11},{12,13},{14,15},{16,17},{18,... | collective-permute-start | bytes 115208 | tf_op jit(solution)/shard_map/ppermute | solution.py:28
  16.5 2.0 collective-permute-start.2
  18.5 1.8 slice_reduce_fusion.30
  20.3 1.4 slice_reduce_fusion.29
  23.3 1.7 maximum_convert_fusion.x_ref
  25.0 10.9 %fusion.1 = f32[512,1280]{1,0:T(8,128)} fusion(f32[544,1280]{1,0:T(8,128)S(1)} %maximum_convert_fusion.x_ref, f32[1280]{0:T(1024)S(1)} %get-tuple-element.45, f32[1280]{0:T(1024)S(1)} %get-tuple-element.16, f32[1280]{0:T(1024)S(1)} %get-tuple-element.17, f32[1280]{0:T(1024)S(1)} %get-tuple-element.18, f32[1280]{0:T(1024)S(1)} %get-tuple-element.19, ...), kind=kLoop, calls=%fused_computation.5 | loop fusion | flops 40632320 | bytes 84049920 | tf_op jit(solution)/shard_map/mul | solution.py:178
  38.0 38.4 %all-gather.2.cloned.1.call-done = bf16[1280,2560]{1,0:T(8,128)(2,1)} async-done(((bf16[80,2560]{1,0:T(8,128)(2,1)}), bf16[1280,2560]{1,0:T(8,128)(2,1)}) %all-gather.2.cloned.1.call-update) | async-done | bytes 6553616 | tf_op jit(solution)/shard_map/all_gather | solution.py:172
  76.4 7.7 %convolution_convert_fusion.1.kv_ref = bf16[512,2560]{1,0:T(8,128)(2,1)S(1)} fusion(bf16[1280,2560]{1,0:T(8,128)(2,1)} %all-gather.2.cloned.1.call-done, f32[512,1280]{1,0:T(8,128)} %fusion.1, bf16[1,512,1280]{2,1,0:T(8,128)(2,1)} %param.8), kind=kOutput, calls=%fused_computation.1 | convolution fusion | flops 3361341440 | bytes 13107200 | tf_op jit(solution)/shard_map/dot_general | solution.py:191
  84.9 1.6 copy-done
  88.8 1.5 collective-permute-start.4
  90.3 2.8 %collective-permute-done.4 = f32[16,4,2,16]{3,2,1,0:T(2,128)S(1)} collective-permute-done((f32[16,4,2,16]{3,2,1,0:T(2,128)S(1)}, f32[16,4,2,16]{3,2,1,0:T(2,128)S(1)}, u32[]{:S(2)}, u32[]{:S(2)}) %collective-permute-start.4) | collective-permute-done | bytes 8224 | tf_op jit(solution)/shard_map/ppermute | solution.py:21
  93.4 1.3 copy-done.3
  94.7 1.3 copy-done.5
  96.0 2.9 %shard_map.120 = (bf16[512,2560]{1,0:T(8,128)(2,1)S(1)}, f32[32,1280]{1,0:T(8,128)S(1)}) custom-call(f32[512,640]{1,0:T(8,128)S(1)} %copy-done.3, f32[512,640]{1,0:T(8,128)S(1)} %copy-done.5, f32[16,128]{1,0:T(8,128)S(1)} %add.178.s_ref, bf16[512,2560]{1,0:T(8,128)(2,1)} %copy-done, bf16[5,128,256]{2,1,0:T(8,128)(2,1)S(1)} %get-tuple-element.58.q_ref, ...), custom_call_target="tpu_custom_call" | custom-call | tf_op jit(solution)/shard_map/pallas_call | solution.py:209
  99.6 1.5 copy-done.8
  101.1 5.7 %convolution_convert_fusion = bf16[1280,2560]{1,0:T(8,128)(2,1)} fusion(bf16[512,2560]{1,0:T(8,128)(2,1)S(1)} %get-tuple-element.13, f32[512,1280]{1,0:T(8,128)S(1)} %copy-done.9, bf16[1,512,1280]{2,1,0:T(8,128)(2,1)S(1)} %copy-done.10), kind=kOutput, calls=%fused_computation | convolution fusion | flops 3363307520 | bytes 13107200 | tf_op jit(solution)/shard_map/dot_general | solution.py:220
  106.8 9.8 %multiply_multiply_fusion = (f32[512,1280]{1,0:T(8,128)S(1)}, f32[512,1280]{1,0:T(8,128)}) fusion(f32[512,1280]{1,0:T(8,128)} %fusion.1, bf16[512,2560]{1,0:T(8,128)(2,1)} %copy-done.8, bf16[1280,2560]{1,0:T(8,128)(2,1)} %all-gather.2.cloned.1.call-done), kind=kOutput, calls=%fused_computation.65 | convolution fusion | flops 3360686080 | bytes 17039360 | tf_op jit(solution)/shard_map/dot_general | solution.py:231
  116.6 13.7 %shard_map.122 = f32[32,1280]{1,0:T(8,128)S(1)} custom-call(f32[512,1280]{1,0:T(8,128)S(1)} %get-tuple-element.55.g_ref, f32[544,1280]{1,0:T(8,128)S(1)} %maximum_convert_fusion.x_ref), custom_call_target="tpu_custom_call" | custom-call | tf_op jit(solution)/shard_map/pallas_call | solution.py:237
  130.4 1.4 collective-permute-done.7
  132.2 5.9 %collective-permute-done.8 = f32[32,1280]{1,0:T(8,128)S(1)} collective-permute-done((f32[32,1280]{1,0:T(8,128)S(1)}, f32[32,1280]{1,0:T(8,128)S(1)}, u32[]{:S(2)}, u32[]{:S(2)}) %collective-permute-start.8) | collective-permute-done | bytes 163872 | tf_op jit(solution)/shard_map/ppermute | solution.py:55
  138.1 1.3 collective-permute-start.9
  139.4 1.3 collective-permute-start.6
  140.7 4.6 %collective-permute-start.5 = (f32[15,1280]{1,0:T(8,128)S(1)}, f32[15,1280]{1,0:T(8,128)S(1)}, u32[]{:S(2)}, u32[]{:S(2)}) collective-permute-start(f32[15,1280]{1,0:T(8,128)S(1)} %get-tuple-element.46), channel_id=1, source_target_pairs={{0,1},{2,3},{4,5},{6,7},{8,9},{10,11},{12,13},{14,15},{16,17},{18,... | collective-permute-start | bytes 230408 | tf_op jit(solution)/shard_map/ppermute | solution.py:28
  146.0 7.4 %collective-permute-done.9 = f32[32,1280]{1,0:T(8,128)S(1)} collective-permute-done((f32[32,1280]{1,0:T(8,128)S(1)}, f32[32,1280]{1,0:T(8,128)S(1)}, u32[]{:S(2)}, u32[]{:S(2)}) %collective-permute-start.9) | collective-permute-done | bytes 163872 | tf_op jit(solution)/shard_map/ppermute | solution.py:55
  153.9 19.5 %collective-permute-done.10 = f32[32,1280]{1,0:T(8,128)S(1)} collective-permute-done((f32[32,1280]{1,0:T(8,128)S(1)}, f32[32,1280]{1,0:T(8,128)S(1)}, u32[]{:S(2)}, u32[]{:S(2)}) %collective-permute-start.10) | collective-permute-done | bytes 163872 | tf_op jit(solution)/shard_map/ppermute | solution.py:55
  173.4 1.5 collective-permute-start.11
  175.0 22.7 %reduce-scatter.2.cloned.1.call-done = bf16[80,2560]{1,0:T(8,128)(2,1)} async-done(((bf16[1280,2560]{1,0:T(8,128)(2,1)}), bf16[80,2560]{1,0:T(8,128)(2,1)}) %reduce-scatter.2.cloned.1.call-update) | async-done | bytes 409616 | tf_op jit(solution)/shard_map/reduce_scatter | solution.py:223
  197.6 1.5 collective-permute-start.12
  199.7 1.3 multiply_reduce_fusion
  201.1 1.7 copy-done.1
  202.8 7.5 %shard_map.121 = bf16[512,1280]{1,0:T(8,128)(2,1)} custom-call(f32[32,1280]{1,0:T(8,128)S(1)} %concatenate.26.taps_ref, f32[544,1280]{1,0:T(8,128)S(1)} %maximum_maximum_fusion.g_ref, f32[512,1280]{1,0:T(8,128)S(1)} %copy-done.1), custom_call_target="tpu_custom_call" | custom-call | tf_op jit(solution)/shard_map/pallas_call | solution.py:255
  (77 shorter events, 12.9 us)
Async XLA Ops:
  7.2 69.2 %all-gather.2.cloned.1.call-start = ((), (), s32[]{:S(2)}) async-start(), calls=%async_computation.1 | async-start | bytes 6963200 | tf_op jit(solution)/shard_map/all_gather | solution.py:172
  7.9 17.1 %copy-start.13 = (f32[1280]{0:T(1024)S(1)}, f32[1280]{0:T(1024)}, u32[]{:S(2)}) copy-start(f32[1280]{0:T(1024)} %param.10) | copy-start | bytes 15364
  7.9 189.7 %reduce-scatter.2.cloned.1.call-start = ((), (), s32[]{:S(2)}) async-start(), calls=%async_computation.2 | async-start | bytes 6963200 | tf_op jit(solution)/shard_map/reduce_scatter | solution.py:223
  8.8 14.5 %collective-permute-start.1 = (bf16[15,1280]{1,0:T(8,128)(2,1)S(1)}, bf16[15,1280]{1,0:T(8,128)(2,1)S(1)}, u32[]{:S(2)}, u32[]{:S(2)}) collective-permute-start(bf16[15,1280]{1,0:T(8,128)(2,1)S(1)} %get-tuple-element.49), channel_id=1, source_target_pairs={{1,0},{3,2},{5,4},{7,6},{9,8},{11,10},{13,12},{15,14},{17,16},{19,... | collective-permute-start | bytes 115208 | tf_op jit(solution)/shard_map/ppermute | solution.py:29
  10.1 13.2 %collective-permute-start = (bf16[15,1280]{1,0:T(8,128)(2,1)S(1)}, bf16[15,1280]{1,0:T(8,128)(2,1)S(1)}, u32[]{:S(2)}, u32[]{:S(2)}) collective-permute-start(bf16[15,1280]{1,0:T(8,128)(2,1)S(1)} %get-tuple-element.48), channel_id=1, source_target_pairs={{0,1},{2,3},{4,5},{6,7},{8,9},{10,11},{12,13},{14,15},{16,17},{18,... | collective-permute-start | bytes 115208 | tf_op jit(solution)/shard_map/ppermute | solution.py:28
  16.4 19.5 %collective-permute-start.3 = (bf16[16,1280]{1,0:T(8,128)(2,1)S(1)}, bf16[16,1280]{1,0:T(8,128)(2,1)S(1)}, u32[]{:S(2)}, u32[]{:S(2)}) collective-permute-start(bf16[16,1280]{1,0:T(8,128)(2,1)S(1)} %bitcast_multiply_fusion.2), channel_id=1, source_target_pairs={{0,1},{1,0},{2,3},{3,2},{4,5},{5,4},{6,7},{7,6},{8,9},{9,8},{10,11... | collective-permute-start | bytes 122888 | tf_op jit(solution)/shard_map/ppermute | solution.py:21
  16.5 20.2 %collective-permute-start.2 = (bf16[16,1280]{1,0:T(8,128)(2,1)}, bf16[16,1280]{1,0:T(8,128)(2,1)S(1)}, u32[]{:S(2)}, u32[]{:S(2)}) collective-permute-start(bf16[16,1280]{1,0:T(8,128)(2,1)} %bitcast.39), channel_id=1, source_target_pairs={{0,1},{1,0},{2,3},{3,2},{4,5},{5,4},{6,7},{7,6},{8,9},{9,8},{10,11... | collective-permute-start | bytes 122888 | tf_op jit(solution)/shard_map/ppermute | solution.py:21
  84.9 1.6 copy-start
  86.5 1.1 copy-start.2
  87.6 1.1 copy-start.4
  88.8 4.3 %collective-permute-start.4 = (f32[16,4,2,16]{3,2,1,0:T(2,128)S(1)}, f32[16,4,2,16]{3,2,1,0:T(2,128)S(1)}, u32[]{:S(2)}, u32[]{:S(2)}) collective-permute-start(f32[16,4,2,16]{3,2,1,0:T(2,128)S(1)} %reshape.123), channel_id=1, source_target_pairs={{0,1},{1,0},{2,3},{3,2},{4,5},{5,4},{6,7},{7,6},{8,9},{9,8},{10,11... | collective-permute-start | bytes 24584 | tf_op jit(solution)/shard_map/ppermute | solution.py:21
  93.4 1.3 copy-start.3
  94.7 1.3 copy-start.5
  96.0 5.1 %copy-start.9 = (f32[512,1280]{1,0:T(8,128)S(1)}, f32[512,1280]{1,0:T(8,128)}, u32[]{:S(2)}) copy-start(f32[512,1280]{1,0:T(8,128)} %fusion.1) | copy-start | bytes 7864324
  96.0 5.1 %copy-start.10 = (bf16[1,512,1280]{2,1,0:T(8,128)(2,1)S(1)}, bf16[1,512,1280]{2,1,0:T(8,128)(2,1)}, u32[]{:S(2)}) copy-start(bf16[1,512,1280]{2,1,0:T(8,128)(2,1)} %param.8) | copy-start | bytes 3932164
  98.9 0.7 copy-start.6
  99.6 1.5 copy-start.8
  116.6 28.7 %copy-start.7 = (f32[32,1280]{1,0:T(8,128)S(1)}, f32[32,1280]{1,0:T(8,128)}, u32[]{:S(2)}) copy-start(f32[32,1280]{1,0:T(8,128)} %copy-done.6) | copy-start | bytes 491524
  130.3 1.5 collective-permute-start.7
  131.8 6.3 %collective-permute-start.8 = (f32[32,1280]{1,0:T(8,128)S(1)}, f32[32,1280]{1,0:T(8,128)S(1)}, u32[]{:S(2)}, u32[]{:S(2)}) collective-permute-start(f32[32,1280]{1,0:T(8,128)S(1)} %add.180), channel_id=1, source_target_pairs={{0,4},{2,6},{4,0},{6,2},{8,12},{10,14},{12,8},{14,10},{16,20},{18,... | collective-permute-start | bytes 491528 | tf_op jit(solution)/shard_map/ppermute | solution.py:55
  138.1 15.3 %collective-permute-start.9 = (f32[32,1280]{1,0:T(8,128)S(1)}, f32[32,1280]{1,0:T(8,128)S(1)}, u32[]{:S(2)}, u32[]{:S(2)}) collective-permute-start(f32[32,1280]{1,0:T(8,128)S(1)} %add.181), channel_id=1, source_target_pairs={{0,8},{2,10},{4,12},{6,14},{8,0},{10,2},{12,4},{14,6},{16,24},{18,... | collective-permute-start | bytes 491528 | tf_op jit(solution)/shard_map/ppermute | solution.py:55
  139.4 14.2 %collective-permute-start.6 = (f32[15,1280]{1,0:T(8,128)S(1)}, f32[15,1280]{1,0:T(8,128)S(1)}, u32[]{:S(2)}, u32[]{:S(2)}) collective-permute-start(f32[15,1280]{1,0:T(8,128)S(1)} %get-tuple-element.47), channel_id=1, source_target_pairs={{1,0},{3,2},{5,4},{7,6},{9,8},{11,10},{13,12},{15,14},{17,16},{19,... | collective-permute-start | bytes 230408 | tf_op jit(solution)/shard_map/ppermute | solution.py:29
  140.7 12.9 %collective-permute-start.5 = (f32[15,1280]{1,0:T(8,128)S(1)}, f32[15,1280]{1,0:T(8,128)S(1)}, u32[]{:S(2)}, u32[]{:S(2)}) collective-permute-start(f32[15,1280]{1,0:T(8,128)S(1)} %get-tuple-element.46), channel_id=1, source_target_pairs={{0,1},{2,3},{4,5},{6,7},{8,9},{10,11},{12,13},{14,15},{16,17},{18,... | collective-permute-start | bytes 230408 | tf_op jit(solution)/shard_map/ppermute | solution.py:28
  146.0 53.1 %collective-permute-start.13 = (f32[16,1280]{1,0:T(8,128)}, f32[16,1280]{1,0:T(8,128)S(1)}, u32[]{:S(2)}, u32[]{:S(2)}) collective-permute-start(f32[16,1280]{1,0:T(8,128)} %slice.295), channel_id=1, source_target_pairs={{0,1},{1,0},{2,3},{3,2},{4,5},{5,4},{6,7},{7,6},{8,9},{9,8},{10,11... | collective-permute-start | bytes 245768 | tf_op jit(solution)/shard_map/ppermute | solution.py:21
  153.4 46.3 %copy-start.11 = (f32[31,1280]{1,0:T(8,128)S(1)}, f32[31,1280]{1,0:T(8,128)}, u32[]{:S(2)}) copy-start(f32[31,1280]{1,0:T(8,128)} %param.9) | copy-start | bytes 476164
  153.4 20.0 %collective-permute-start.10 = (f32[32,1280]{1,0:T(8,128)S(1)}, f32[32,1280]{1,0:T(8,128)S(1)}, u32[]{:S(2)}, u32[]{:S(2)}) collective-permute-start(f32[32,1280]{1,0:T(8,128)S(1)} %add.182), channel_id=1, source_target_pairs={{0,16},{2,18},{4,20},{6,22},{8,24},{10,26},{12,28},{14,30},{16,0},... | collective-permute-start | bytes 491528 | tf_op jit(solution)/shard_map/ppermute | solution.py:55
  173.4 26.3 %collective-permute-start.11 = (f32[32,1280]{1,0:T(8,128)S(1)}, f32[32,1280]{1,0:T(8,128)S(1)}, u32[]{:S(2)}, u32[]{:S(2)}) collective-permute-start(f32[32,1280]{1,0:T(8,128)S(1)} %add.183), channel_id=1, source_target_pairs={{0,1},{1,0},{2,3},{3,2},{4,5},{5,4},{6,7},{7,6},{8,9},{9,8},{10,11... | collective-permute-start | bytes 491528 | tf_op jit(solution)/shard_map/ppermute | solution.py:55
  197.6 12.6 %collective-permute-start.12 = (bf16[80,2560]{1,0:T(8,128)(2,1)}, bf16[80,2560]{1,0:T(8,128)(2,1)S(1)}, u32[]{:S(2)}, u32[]{:S(2)}) collective-permute-start(bf16[80,2560]{1,0:T(8,128)(2,1)} %reduce-scatter.2.cloned.1.call-done), channel_id=1, source_target_pairs={{0,1},{1,0},{2,3},{3,2},{4,5},{5,4},{6,7},{7,6},{8,9},{9,8},{10,11... | collective-permute-start | bytes 1228808 | tf_op jit(solution)/shard_map/ppermute | solution.py:21
  201.1 1.7 copy-start.1
  202.8 7.5 %copy-start.12 = (bf16[80,2560]{1,0:T(8,128)(2,1)S(1)}, bf16[80,2560]{1,0:T(8,128)(2,1)}, u32[]{:S(2)}) copy-start(bf16[80,2560]{1,0:T(8,128)(2,1)} %reduce-scatter.2.cloned.1.call-done) | copy-start | bytes 1228804
Sparse Core Ops, SparseCore 0:
  10.3 66.0 all-gather.1
  106.9 90.7 reduce-scatter.1

commit v2 on v1

--- a/solution.py
+++ b/solution.py
@@ -11,6 +11,8 @@
 PACK = 4
 LANES = 128
 VMEM_BYTES = 48 * 1024 * 1024
+GATHER_GROUPS = (("offload", 0, 10),)
+SCATTER_GROUPS = (("ctx", 0, 5), ("dp", 5, 10))
 F32 = jnp.float32
 BF16 = jnp.bfloat16
 
@@ -23,6 +25,13 @@
 
 def rims(block, width):
     count = lax.axis_size("ctx")
+    if count == 2:
+        first = lax.axis_index("ctx") == 0
+        other = exchange(
+            jnp.where(first, block[block.shape[0] - width :], block[:width]), "ctx", 0
+        )
+        zero = jnp.zeros_like(other)
+        return jnp.where(first, zero, other), jnp.where(first, other, zero)
     forward = [(i, i + 1) for i in range(count - 1)]
     backward = [(i + 1, i) for i in range(count - 1)]
     low = lax.ppermute(block[block.shape[0] - width :], "ctx", forward)
@@ -57,6 +66,92 @@
     return value
 
 
+def bits_of(axis):
+    count = lax.axis_size(axis)
+    return count.bit_length() - 1
+
+
+def stages(path):
+    dp = [("dp", bit) for bit in range(bits_of("dp"))]
+    ctx = [("ctx", bit) for bit in range(bits_of("ctx"))]
+    first = dp[:1] if path == "ctx" else dp[:2]
+    return first + ctx + dp[len(first) :]
+
+
+def exchange(value, axis, bit):
+    count = lax.axis_size(axis)
+    return lax.ppermute(value, axis, [(i, i ^ (1 << bit)) for i in range(count)])
+
+
+def bit_at(axis, bit):
+    return (lax.axis_index(axis) >> bit) & 1
+
+
+def plain_sizes():
+    return all(lax.axis_size(a) == 1 << bits_of(a) for a in ("dp", "ctx"))
+
+
+def half_dim(value, axis, bit, open_bits):
+    if axis == "ctx":
+        return value.ndim - 1
+    return len(open_bits) - 1 - sorted(open_bits).index(bit)
+
+
+def scatter_sum(value, path):
+    if path == "offload" or not plain_sizes():
+        part = lax.psum_scatter(value, "dp", scatter_dimension=0, tiled=True)
+        if lax.axis_size("ctx") == 2:
+            return part.astype(F32) + shifted(part, "ctx", 1).astype(F32), []
+        return lax.psum(part.astype(F32), "ctx"), []
+    sums = []
+    open_bits = list(range(bits_of("dp")))
+    rows, cols = value.shape
+    value = value.reshape([2] * len(open_bits) + [rows // lax.axis_size("dp"), cols])
+    for axis, bit in stages(path):
+        dim = half_dim(value, axis, bit, open_bits)
+        half = value.shape[dim] // 2
+        mine = bit_at(axis, bit)
+        keep = lax.dynamic_slice_in_dim(value, mine * half, half, dim)
+        send = lax.dynamic_slice_in_dim(value, (1 - mine) * half, half, dim)
+        if axis == "dp":
+            keep, send = jnp.squeeze(keep, dim), jnp.squeeze(send, dim)
+            open_bits.remove(bit)
+        value = (keep.astype(F32) + exchange(send, axis, bit).astype(F32)).astype(BF16)
+        sums.append(value)
+    for bit in reversed(range(bits_of("ctx"))):
+        other = exchange(value, "ctx", bit)
+        value = jnp.where(
+            bit_at("ctx", bit) == 0,
+            jnp.concatenate([value, other], axis=1),
+            jnp.concatenate([other, value], axis=1),
+        )
+    return value.astype(F32), sums
+
+
+def gather_rows(value, path):
+    if path == "offload" or not plain_sizes():
+        return lax.all_gather(value, "dp", axis=0, tiled=True)
+    rows, cols = value.shape
+    for bit in range(bits_of("ctx")):
+        half = value.shape[1] // 2
+        value = lax.dynamic_slice_in_dim(value, bit_at("ctx", bit) * half, half, 1)
+    open_bits = []
+    for axis, bit in reversed(stages(path)):
+        other = exchange(value, axis, bit)
+        if axis == "dp":
+            open_bits.append(bit)
+            dim = half_dim(value, axis, bit, open_bits)
+            value, other = jnp.expand_dims(value, dim), jnp.expand_dims(other, dim)
+        else:
+            dim = value.ndim - 1
+        value = jnp.where(
+            bit_at(axis, bit) == 0,
+            jnp.concatenate([value, other], axis=dim),
+            jnp.concatenate([other, value], axis=dim),
+        )
+    return value.reshape(-1, cols)
+
+
 def conv_time(padded, conv_taps, length):
     total = jnp.zeros((length, padded.shape[1]), F32)
     for tap_idx in range(conv_taps.shape[0]):
@@ -74,55 +169,54 @@
     return (rows.astype(F32) * own[None, :, None, :]).astype(BF16).reshape(groups, PACK * tokens, cols)
 
 
-def score_kernel(limit_ref, kv_ref, q_ref, g_ref, e_ref, d_ref, s_ref):
+def scores_of(limit_ref, kv_ref, q_ref, g_ref, j):
     groups, lanes, cols = q_ref.shape
     length = kv_ref.shape[0]
     width = groups * cols
     live = lax.broadcasted_iota(jnp.int32, (length, lanes), 0) < limit_ref[0]
     dims = (((1,), (1,)), ((), ()))
+    keys = kv_ref[:, j * cols : (j + 1) * cols]
+    values = kv_ref[:, width + j * cols : width + (j + 1) * cols]
+    scores = lax.dot_general(keys, q_ref[j], dims, preferred_element_type=F32)
+    dprob = lax.dot_general(values, g_ref[j], dims, preferred_element_type=F32)
+    return jnp.where(live, jnp.exp(scores), 0.0), dprob, keys
+
+
+def score_kernel(limit_ref, kv_ref, q_ref, g_ref, s_ref):
     s_ref[...] = jnp.zeros_like(s_ref)
-    for j in range(groups):
-        keys = kv_ref[:, j * cols : (j + 1) * cols]
-        values = kv_ref[:, width + j * cols : width + (j + 1) * cols]
-        scores = lax.dot_general(keys, q_ref[j], dims, preferred_element_type=F32)
-        exps = jnp.where(live, jnp.exp(scores), 0.0)
-        dprob = lax.dot_general(values, g_ref[j], dims, preferred_element_type=F32)
-        e_ref[:, j * lanes : (j + 1) * lanes] = exps
-        d_ref[:, j * lanes : (j + 1) * lanes] = dprob
+    for j in range(q_ref.shape[0]):
+        exps, dprob, _ = scores_of(limit_ref, kv_ref, q_ref, g_ref, j)
         s_ref[j : j + 1] = jnp.sum(exps, axis=0, keepdims=True)
         s_ref[8 + j : 9 + j] = jnp.sum(exps.astype(BF16).astype(F32) * dprob, axis=0, keepdims=True)
 
 
-def grad_kernel(e_ref, d_ref, s_ref, kv_ref, q_ref, g_ref, kvg_ref, qg_ref):
+def grad_kernel(limit_ref, s_ref, kv_ref, q_ref, g_ref, kvg_ref, qg_ref):
     groups, lanes, cols = q_ref.shape
     width = groups * cols
     tokens = lanes // PACK
     head_dim = cols // PACK
     head_of = lax.broadcasted_iota(jnp.int32, (tokens, cols), 1) // head_dim
     for j in range(groups):
+        exps, dprob, keys = scores_of(limit_ref, kv_ref, q_ref, g_ref, j)
         inverse = 1.0 / s_ref[j : j + 1]
         delta = s_ref[8 + j : 9 + j] * inverse
-        prob = e_ref[:, j * lanes : (j + 1) * lanes] * inverse
-        dscore = (prob * (d_ref[:, j * lanes : (j + 1) * lanes] - delta)).astype(BF16)
+        prob = exps * inverse
+        dscore = (prob * (dprob - delta)).astype(BF16)
         kvg_ref[:, j * cols : (j + 1) * cols] = jnp.dot(
             dscore, q_ref[j], preferred_element_type=F32
         ).astype(BF16)
         kvg_ref[:, width + j * cols : width + (j + 1) * cols] = jnp.dot(
             prob.astype(BF16), g_ref[j], preferred_element_type=F32
         ).astype(BF16)
-        full = lax.dot_general(
-            dscore,
-            kv_ref[:, j * cols : (j + 1) * cols],
-            (((0,), (0,)), ((), ())),
-            preferred_element_type=F32,
-        )
+        full = lax.dot_general(dscore, keys, (((0,), (0,)), ((), ())), preferred_element_type=F32)
         total = jnp.zeros((tokens, cols), F32)
         for h in range(PACK):
             total = total + jnp.where(head_of == h, full[h * tokens : (h + 1) * tokens], 0.0)
         qg_ref[:, j * cols : (j + 1) * cols] = total
 
 
-def taps_kernel(tap_count, g_ref, x_ref, t_ref):
+def taps_kernel(tap_count, g_ref, x_ref, *rest):
+    t_ref = rest[-1]
     length = g_ref.shape[0]
 
     def step(i, sums):
@@ -137,7 +231,8 @@
         t_ref[k : k + 1, :] = jnp.sum(sums[k], axis=0, keepdims=True)
 
 
-def back_kernel(tap_count, taps_ref, g_ref, e_ref, o_ref):
+def back_kernel(tap_count, taps_ref, g_ref, e_ref, *rest):
+    o_ref = rest[-1]
     rows = 64
 
     def step(i, carry):
@@ -153,6 +248,10 @@
 
 def whole_spec():
     return pl.BlockSpec(memory_space=pltpu.VMEM)
+
+
+def any_spec():
+    return pl.BlockSpec(memory_space=pl.ANY)
 
 
 def column_spec(rows):
@@ -169,7 +268,11 @@
     scale = (width // HEADS) ** (-0.5)
     params = pltpu.CompilerParams(vmem_limit_bytes=VMEM_BYTES)
 
-    w_full = lax.all_gather(w_kv, "dp", axis=0, tiled=True)
+    tenth = 2 * width // 10
+    w_groups = [
+        gather_rows(w_kv[:, lo * tenth : hi * tenth], path) for path, lo, hi in GATHER_GROUPS
+    ]
+    w_full = jnp.concatenate(w_groups, axis=1)
     block = frames[0]
     low, high = rims(block, rim)
     tail = -(length + 2 * rim) % 16
@@ -188,16 +291,15 @@
     all_tokens = lanes // PACK
     limit = (frame_len - cycle_pos * length).astype(jnp.int32)
 
-    key_values = jnp.dot(encoded, w_full, preferred_element_type=F32).astype(BF16)
-    exps, dprob, stats = pl.pallas_call(
+    key_values = jnp.concatenate(
+        [jnp.dot(encoded, w, preferred_element_type=F32).astype(BF16) for w in w_groups], axis=1
+    )
+    smem = pl.BlockSpec(memory_space=pltpu.SMEM)
+    stats = pl.pallas_call(
         score_kernel,
-        out_shape=(
-            jax.ShapeDtypeStruct((length, groups * lanes), F32),
-            jax.ShapeDtypeStruct((length, groups * lanes), F32),
-            jax.ShapeDtypeStruct((16, lanes), F32),
-        ),
-        in_specs=[pl.BlockSpec(memory_space=pltpu.SMEM)] + [whole_spec()] * 3,
-        out_specs=(whole_spec(),) * 3,
+        out_shape=jax.ShapeDtypeStruct((16, lanes), F32),
+        in_specs=[smem] + [whole_spec()] * 3,
+        out_specs=whole_spec(),
         compiler_params=params,
     )(limit, key_values, q_pack, g_pack)
     count = lax.axis_size("ctx")
@@ -212,15 +314,25 @@
             jax.ShapeDtypeStruct((length, 2 * width), BF16),
             jax.ShapeDtypeStruct((all_tokens, width), F32),
         ),
-        in_specs=[whole_spec()] * 6,
+        in_specs=[smem] + [whole_spec()] * 4,
         out_specs=(whole_spec(),) * 2,
         compiler_params=params,
-    )(exps, dprob, stats, key_values, q_pack, g_pack)
-
-    w_part = lax.dot_general(
-        encoded, kv_grad, (((0,), (0,)), ((), ())), preferred_element_type=F32
-    ).astype(BF16)
-    w_rows = lax.psum_scatter(w_part, "dp", scatter_dimension=0, tiled=True)
+    )(limit, stats, key_values, q_pack, g_pack)
+
+    w_grads, w_parts, early, late = [], [], [], []
+    for path, lo, hi in SCATTER_GROUPS:
+        w_part = lax.dot_general(
+            encoded,
+            kv_grad[:, lo * tenth : hi * tenth],
+            (((0,), (0,)), ((), ())),
+            preferred_element_type=F32,
+        ).astype(BF16)
+        w_parts.append(w_part)
+        w_sum, sums = scatter_sum(w_part, path)
+        w_grads.append(w_sum)
+        early += sums[:1]
+        late += sums[1:2]
+    w_kv_grad = jnp.concatenate(w_grads, axis=1)
 
     q_parts = q_part.reshape(count, tokens, width)
     q_sum = q_parts[0]
@@ -228,8 +340,9 @@
         q_sum = q_sum + shifted(q_parts[step], "ctx", -step)
     queries_grad = (q_sum * scale).astype(BF16)[None]
 
+    kv_late = lax.optimization_barrier((kv_grad, *w_parts))[0]
     enc_grad = lax.dot_general(
-        kv_grad, w_full, (((1,), (1,)), ((), ())), preferred_element_type=F32
+        kv_late, w_full, (((1,), (1,)), ((), ())), preferred_element_type=F32
     )
     gated_grad = enc_grad * slope
     grad_low, grad_high = rims(gated_grad, rim)
@@ -238,10 +351,15 @@
         functools.partial(taps_kernel, tap_count),
         grid=(width // LANES,),
         out_shape=jax.ShapeDtypeStruct((tap_rows, width), F32),
-        in_specs=[column_spec(length), column_spec(padded.shape[0])],
+        in_specs=[column_spec(length), column_spec(padded.shape[0])] + [any_spec()] * len(early),
         out_specs=column_spec(tap_rows),
         compiler_params=params,
-    )(gated_grad, padded)
+        cost_estimate=pl.CostEstimate(
+            flops=2 * tap_count * length * width,
+            bytes_accessed=4 * tap_count * length * width,
+            transcendentals=0,
+        ),
+    )(gated_grad, padded, *early)
     tap_sums = sum_all(tap_sums)[:tap_count]
     taps_grad = tap_sums * conv_gain
     gain_grad = jnp.sum(tap_sums * conv_taps, axis=0)
@@ -256,15 +374,16 @@
         functools.partial(back_kernel, tap_count),
         grid=(width // LANES,),
         out_shape=jax.ShapeDtypeStruct((length, width), BF16),
-        in_specs=[column_spec(tap_rows), column_spec(padded_grad.shape[0]), column_spec(length)],
+        in_specs=[column_spec(tap_rows), column_spec(padded_grad.shape[0]), column_spec(length)]
+        + [any_spec()] * len(late),
         out_specs=column_spec(length),
         compiler_params=params,
-    )(scaled_taps, padded_grad, enc_grad)[None]
-
-    if count == 2:
-        w_kv_grad = w_rows.astype(F32) + shifted(w_rows, "ctx", 1).astype(F32)
-    else:
-        w_kv_grad = lax.psum(w_rows.astype(F32), "ctx")
+        cost_estimate=pl.CostEstimate(
+            flops=2 * tap_count * length * width,
+            bytes_accessed=4 * tap_count * length * width,
+            transcendentals=0,
+        ),
+    )(scaled_taps, padded_grad, enc_grad, *late)[None]
     return (frames_grad, taps_grad, gain_grad, w_kv_grad, queries_grad)
 
 

time: 219 us -> 197 us (0.90)
  waiting for transfers between devices: 98.8 us -> 83.1 us
  local copies, waits for them, and re-layouts: 17.1 us -> 6.26 us
  matrix products: 23.2 us -> 14.2 us
  starting transfers between devices: 20.5 us -> 26.4 us
  other arithmetic: 18 us -> 23.4 us
    reduce_scatter x1 -> x0, waiting for transfers between devices: 22.7 us -> none  [per_device(): w_rows = lax.psum_scatter(w_part, 'dp', scatter_dimension=0, tiled=True)]
    ppermute x4 -> x14, waiting for transfers between devices: 0.01 us -> 22.5 us  [exchange(): return lax.ppermute(value, axis, [(i, i ^ 1 << bit) for i in range(count)])]
    ppermute x5, waiting for transfers between devices: 34.2 us -> 15 us  [sum_all(): lax.ppermute(value, axis, [(i, i ^ step) for i in range(count)])]
    convert_element_type x0 -> x11, other arithmetic: none -> 13.3 us  [the longest x1 11.7 us: per_device(): encoded = (block.astype(F32) + gated * sigma).astype(BF16)]
    mul x1, other arithmetic: 10.9 us -> 1.16 us  [per_device(): gated_grad = enc_grad * slope]
    unnamed x28 -> x16, local copies, waits for them, and re-layouts: 10.2 us -> 0.64 us
    dot_general x3 -> x4, matrix products: 23.2 us -> 14.2 us  [the longest x1 6.81 us: per_device(): jnp.dot(encoded, w, preferred_element_type=F32).astype(BF16)]
    ppermute x4 -> x14, starting transfers between devices: 12 us -> 16.6 us  [exchange(): return lax.ppermute(value, axis, [(i, i ^ 1 << bit) for i in range(count)])]
  transfers between devices with their start and end apart: 16 -> 24, of which waited for: 7 -> 15; matrix products, arithmetic and copies ran while one was open for 15% -> 16% of each run, Pallas kernels for 10% -> 12%
where the time goes in v2:
time: 197 us; the launch traced here: 196 us
  waiting for transfers between devices  83.1 us (42%)
  Pallas kernels  27 us (14%)
  starting transfers between devices  26.4 us (13%)
  other arithmetic  23.4 us (12%)
  between operations  15.9 us (8%)
  matrix products  14.2 us (7%)
  local copies, waits for them, and re-layouts  6.26 us (3%)
    all_gather x1, waiting for transfers between devices, gather_rows(): return lax.all_gather(value, 'dp', axis=0, tiled=True)  42.1 us
    ppermute x14, waiting for transfers between devices, exchange(): return lax.ppermute(value, axis, [(i, i ^ 1 << bit) for i in range(count)])  22.5 us
    ppermute x14, starting transfers between devices, exchange(): return lax.ppermute(value, axis, [(i, i ^ 1 << bit) for i in range(count)])  16.6 us
    ppermute x5, waiting for transfers between devices, sum_all(): lax.ppermute(value, axis, [(i, i ^ step) for i in range(count)])  15 us
    pallas_call x1, Pallas kernels, per_device(): pl.pallas_call(functools.partial(taps_kernel, tap_count), grid=(width //...  14.4 us
    convert_element_type x1, other arithmetic, per_device(): encoded = (block.astype(F32) + gated * sigma).astype(BF16)  11.7 us
    pallas_call x1, Pallas kernels, per_device(): pl.pallas_call(functools.partial(back_kernel, tap_count), grid=(width //...  9.87 us
    dot_general x1, matrix products, per_device(): jnp.dot(encoded, w, preferred_element_type=F32).astype(BF16)  6.81 us
  transfers between devices with their start and end apart: 24, of which 15 were waited for; matrix products, arithmetic and copies ran while one was open for 16% of the time, Pallas kernels for 12%

profile of v2, /device:TPU:0, one launch (start us, length us, event | category | flops | bytes accessed | tf_op | source)
XLA Modules:
  0.0 196.2 jit_solution(480377176709594222)
XLA Ops:
  8.8 3.0 %collective-permute-start = (bf16[15,1280]{1,0:T(8,128)(2,1)S(1)}, bf16[15,1280]{1,0:T(8,128)(2,1)S(1)}, u32[]{:S(2)}, u32[]{:S(2)}) collective-permute-start(bf16[15,1280]{1,0:T(8,128)(2,1)S(1)} %select_bitcast_fusion), channel_id=1, source_target_pairs={{0,1},{1,0},{2,3},{3,2},{4,5},{5,4},{6,7},{7,6},{8,9},{9,8},{10,11... | collective-permute-start | bytes 115208 | tf_op jit(solution)/shard_map/ppermute | solution.py:83
  13.4 2.0 %collective-permute-start.1 = (bf16[16,1280]{1,0:T(8,128)(2,1)}, bf16[16,1280]{1,0:T(8,128)(2,1)S(1)}, u32[]{:S(2)}, u32[]{:S(2)}) collective-permute-start(bf16[16,1280]{1,0:T(8,128)(2,1)} %bitcast.88), channel_id=1, source_target_pairs={{0,1},{1,0},{2,3},{3,2},{4,5},{5,4},{6,7},{7,6},{8,9},{9,8},{10,11... | collective-permute-start | bytes 122888 | tf_op jit(solution)/shard_map/ppermute | solution.py:23
  15.4 1.7 slice_reduce_fusion.30
  20.1 1.8 maximum_convert_fusion.x_ref
  22.0 11.7 %add_convert_fusion = (bf16[512,1280]{1,0:T(8,128)(2,1)}, f32[512,1280]{1,0:T(8,128)}) fusion(bf16[1,512,1280]{2,1,0:T(8,128)(2,1)S(1)} %copy-done.2, f32[544,1280]{1,0:T(8,128)S(1)} %maximum_convert_fusion.x_ref, f32[1280]{0:T(1024)S(1)} %get-tuple-element.41, f32[1280]{0:T(1024)S(1)} %get-tuple-element.12, f32[1280]{0:T(1024)S(1)} %get-tuple-element.13, ...), kind=kLoop, calls=%fused_computation.71 | loop fusion | flops 45219840 | bytes 86671360 | tf_op jit(solution)/shard_map/convert_element_type | solution.py:283
  34.3 42.1 %all-gather.2.cloned.1.call-done = bf16[1280,2560]{1,0:T(8,128)(2,1)} async-done(((bf16[80,2560]{1,0:T(8,128)(2,1)}), bf16[1280,2560]{1,0:T(8,128)(2,1)}) %all-gather.2.cloned.1.call-update) | async-done | bytes 6553616 | tf_op jit(solution)/shard_map/all_gather | solution.py:133
  76.4 6.8 %convolution_convert_fusion.2.kv_ref = bf16[512,2560]{1,0:T(8,128)(2,1)S(1)} fusion(bf16[512,1280]{1,0:T(8,128)(2,1)} %get-tuple-element.42, bf16[1280,2560]{1,0:T(8,128)(2,1)} %all-gather.2.cloned.1.call-done), kind=kOutput, calls=%fused_computation.2 | convolution fusion | flops 3356753920 | bytes 10485760 | tf_op jit(solution)/shard_map/dot_general | solution.py:295
  84.2 1.5 collective-permute-start.3
  85.9 2.7 %collective-permute-done.3 = f32[16,4,2,16]{3,2,1,0:T(2,128)S(1)} collective-permute-done((f32[16,4,2,16]{3,2,1,0:T(2,128)S(1)}, f32[16,4,2,16]{3,2,1,0:T(2,128)S(1)}, u32[]{:S(2)}, u32[]{:S(2)}) %collective-permute-start.3) | collective-permute-done | bytes 8224 | tf_op jit(solution)/shard_map/ppermute | solution.py:23
  88.8 1.8 shard_map.120
  90.7 1.9 convolution_convert_fusion.1
  92.6 1.9 convolution_convert_fusion
  96.3 3.6 %fusion.48.e_ref = f32[512,1280]{1,0:T(8,128)S(1)} fusion(bf16[512,2560]{1,0:T(8,128)(2,1)S(1)} %get-tuple-element.9, bf16[1280,2560]{1,0:T(8,128)(2,1)S(1)} %bitcast.90), kind=kOutput, calls=%fused_computation.166 | convolution fusion | flops 3355443200 | bytes 11796480 | tf_op jit(solution)/shard_map/dot_general | solution.py:344
  101.1 1.5 collective-permute-start.4
  104.1 14.4 %shard_map.122 = f32[32,1280]{1,0:T(8,128)S(1)} custom-call(f32[512,1280]{1,0:T(8,128)S(1)} %multiply_multiply_fusion.g_ref, f32[544,1280]{1,0:T(8,128)} %copy-done, bf16[2,2,2,80,1280]{4,3,2,1,0:T(8,128)(2,1)S(1)} %copy.23.rest_0_, bf16[2,2,2,80,1280]{4,3,2,1,0:T(8,128)(2,1)S(1)} %fusion.rest_1_), custom_call_target="tpu_custom_call" | custom-call | flops 40632320 | bytes 81264640 | tf_op jit(solution)/shard_map/pallas_call | solution.py:350
  120.7 1.5 collective-permute-start.8
  122.2 4.9 %collective-permute-done.10 = f32[32,1280]{1,0:T(8,128)S(1)} collective-permute-done((f32[32,1280]{1,0:T(8,128)S(1)}, f32[32,1280]{1,0:T(8,128)S(1)}, u32[]{:S(2)}, u32[]{:S(2)}) %collective-permute-start.10) | collective-permute-done | bytes 163872 | tf_op jit(solution)/shard_map/ppermute | solution.py:64
  128.6 1.9 maximum_maximum_fusion.g_ref
  130.6 1.5 collective-permute-start.6
  132.6 1.9 collective-permute-start.12
  135.1 5.7 %collective-permute-done.12 = f32[32,1280]{1,0:T(8,128)S(1)} collective-permute-done((f32[32,1280]{1,0:T(8,128)S(1)}, f32[32,1280]{1,0:T(8,128)S(1)}, u32[]{:S(2)}, u32[]{:S(2)}) %collective-permute-start.12) | collective-permute-done | bytes 163872 | tf_op jit(solution)/shard_map/ppermute | solution.py:64
  142.3 1.6 collective-permute-done.8
  144.2 1.5 collective-permute-start.18
  145.7 6.1 %collective-permute-done.6 = bf16[2,2,2,80,640]{4,3,0,1,2:T(8,128)(2,1)S(1)} collective-permute-done((bf16[2,2,2,80,640]{4,3,0,1,2:T(8,128)(2,1)S(1)}, bf16[2,2,2,80,640]{4,3,0,1,2:T(8,128)(2,1)S(1)}, u32[]{:S(2)}, u32[]{:S(2)}) %collective-permute-start.6) | collective-permute-done | bytes 819232 | tf_op jit(solution)/shard_map/ppermute | solution.py:83
  152.7 2.7 %collective-permute-done.13 = f32[32,1280]{1,0:T(8,128)S(1)} collective-permute-done((f32[32,1280]{1,0:T(8,128)S(1)}, f32[32,1280]{1,0:T(8,128)S(1)}, u32[]{:S(2)}, u32[]{:S(2)}) %collective-permute-start.13) | collective-permute-done | bytes 163872 | tf_op jit(solution)/shard_map/ppermute | solution.py:64
  156.7 9.9 %shard_map.121 = bf16[512,1280]{1,0:T(8,128)(2,1)} custom-call(f32[32,1280]{1,0:T(8,128)S(1)} %concatenate.44.taps_ref, f32[544,1280]{1,0:T(8,128)} %maximum_maximum_fusion.g_ref, f32[512,1280]{1,0:T(8,128)S(1)} %fusion.48.e_ref, bf16[2,2,2,80,640]{4,3,2,1,0:T(8,128)(2,1)S(1)} %copy.22.rest_0_, bf16[2,2,80,1280]{3,2,1,0:T(8,128)(2,1)S(1)} %fusion.33.rest_1_), custom_call_target="tpu_custom_call" | custom-call | flops 40632320 | bytes 81264640 | tf_op jit(solution)/shard_map/pallas_call | solution.py:373
  169.1 5.5 %collective-permute-done.19 = bf16[2,80,640]{2,1,0:T(8,128)(2,1)S(1)} collective-permute-done((bf16[2,80,640]{2,1,0:T(8,128)(2,1)S(1)}, bf16[2,80,640]{2,1,0:T(8,128)(2,1)S(1)}, u32[]{:S(2)}, u32[]{:S(2)}) %collective-permute-start.19) | collective-permute-done | bytes 204832 | tf_op jit(solution)/shard_map/ppermute | solution.py:83
  174.9 1.9 collective-permute-done.15
  177.9 2.7 %collective-permute-done.20 = bf16[80,640]{1,0:T(8,128)(2,1)S(1)} collective-permute-done((bf16[80,640]{1,0:T(8,128)(2,1)S(1)}, bf16[80,640]{1,0:T(8,128)(2,1)S(1)}, u32[]{:S(2)}, u32[]{:S(2)}) %collective-permute-start.20) | collective-permute-done | bytes 102432 | tf_op jit(solution)/shard_map/ppermute | solution.py:83
  180.6 1.5 collective-permute-start.21
  183.6 1.5 collective-permute-start.17
  185.4 3.0 %collective-permute-done.17 = bf16[80,640]{1,0:T(8,128)(2,1)S(1)} collective-permute-done((bf16[80,640]{1,0:T(8,128)(2,1)S(1)}, bf16[80,640]{1,0:T(8,128)(2,1)S(1)}, u32[]{:S(2)}, u32[]{:S(2)}) %collective-permute-start.17) | collective-permute-done | bytes 102432 | tf_op jit(solution)/shard_map/ppermute | solution.py:83
  (110 shorter events, 26.2 us)
Async XLA Ops:
  7.2 69.2 %all-gather.2.cloned.1.call-start = ((), (), s32[]{:S(2)}) async-start(), calls=%async_computation | async-start | bytes 6963200 | tf_op jit(solution)/shard_map/all_gather | solution.py:133
  7.9 14.1 %copy-start.2 = (bf16[1,512,1280]{2,1,0:T(8,128)(2,1)S(1)}, bf16[1,512,1280]{2,1,0:T(8,128)(2,1)}, u32[]{:S(2)}) copy-start(bf16[1,512,1280]{2,1,0:T(8,128)(2,1)} %param.8) | copy-start | bytes 3932164
  7.9 14.1 %copy-start.5 = (f32[1280]{0:T(1024)S(1)}, f32[1280]{0:T(1024)}, u32[]{:S(2)}) copy-start(f32[1280]{0:T(1024)} %param.10) | copy-start | bytes 15364
  8.8 11.3 %collective-permute-start = (bf16[15,1280]{1,0:T(8,128)(2,1)S(1)}, bf16[15,1280]{1,0:T(8,128)(2,1)S(1)}, u32[]{:S(2)}, u32[]{:S(2)}) collective-permute-start(bf16[15,1280]{1,0:T(8,128)(2,1)S(1)} %select_bitcast_fusion), channel_id=1, source_target_pairs={{0,1},{1,0},{2,3},{3,2},{4,5},{5,4},{6,7},{7,6},{8,9},{9,8},{10,11... | collective-permute-start | bytes 115208 | tf_op jit(solution)/shard_map/ppermute | solution.py:83
  13.4 20.4 %collective-permute-start.2 = (bf16[16,1280]{1,0:T(8,128)(2,1)S(1)}, bf16[16,1280]{1,0:T(8,128)(2,1)S(1)}, u32[]{:S(2)}, u32[]{:S(2)}) collective-permute-start(bf16[16,1280]{1,0:T(8,128)(2,1)S(1)} %bitcast_multiply_fusion.2), channel_id=1, source_target_pairs={{0,1},{1,0},{2,3},{3,2},{4,5},{5,4},{6,7},{7,6},{8,9},{9,8},{10,11... | collective-permute-start | bytes 122888 | tf_op jit(solution)/shard_map/ppermute | solution.py:23
  13.4 20.5 %collective-permute-start.1 = (bf16[16,1280]{1,0:T(8,128)(2,1)}, bf16[16,1280]{1,0:T(8,128)(2,1)S(1)}, u32[]{:S(2)}, u32[]{:S(2)}) collective-permute-start(bf16[16,1280]{1,0:T(8,128)(2,1)} %bitcast.88), channel_id=1, source_target_pairs={{0,1},{1,0},{2,3},{3,2},{4,5},{5,4},{6,7},{7,6},{8,9},{9,8},{10,11... | collective-permute-start | bytes 122888 | tf_op jit(solution)/shard_map/ppermute | solution.py:23
  22.0 11.8 %copy-start = (f32[544,1280]{1,0:T(8,128)}, f32[544,1280]{1,0:T(8,128)S(1)}, u32[]{:S(2)}) copy-start(f32[544,1280]{1,0:T(8,128)S(1)} %maximum_convert_fusion.x_ref) | copy-start | bytes 8355844
  84.2 4.3 %collective-permute-start.3 = (f32[16,4,2,16]{3,2,1,0:T(2,128)S(1)}, f32[16,4,2,16]{3,2,1,0:T(2,128)S(1)}, u32[]{:S(2)}, u32[]{:S(2)}) collective-permute-start(f32[16,4,2,16]{3,2,1,0:T(2,128)S(1)} %reshape.147), channel_id=1, source_target_pairs={{0,1},{1,0},{2,3},{3,2},{4,5},{5,4},{6,7},{7,6},{8,9},{9,8},{10,11... | collective-permute-start | bytes 24584 | tf_op jit(solution)/shard_map/ppermute | solution.py:23
  88.8 1.9 copy-start.3
  92.6 3.1 %slice-start = ((s8[6553600]{0:T(1024)(128)(4,1)}), s8[4194304]{0:T(1024)(128)(4,1)S(1)}, s32[]{:S(2)}) async-start(s8[6553600]{0:T(1024)(128)(4,1)} %bitcast.89), calls=%async_computation.1 | async-start | bytes 8388608
  94.5 1.7 slice-start.1
  94.9 8.2 %collective-permute-start.5 = (bf16[2,2,2,80,1280]{4,3,0,1,2:T(8,128)(2,1)S(1)}, bf16[2,2,2,80,1280]{4,3,0,1,2:T(8,128)(2,1)S(1)}, u32[]{:S(2)}, u32[]{:S(2)}) collective-permute-start(bf16[2,2,2,80,1280]{4,3,0,1,2:T(8,128)(2,1)S(1)} %bitcast.83), channel_id=1, source_target_pairs={{0,2},{2,0},{4,6},{6,4},{8,10},{10,8},{12,14},{14,12},{16,18},{18,... | collective-permute-start | bytes 4915208 | tf_op jit(solution)/shard_map/ppermute | solution.py:83
  95.1 4.8 %copy-start.1 = (f32[512,1280]{1,0:T(8,128)S(1)}, f32[512,1280]{1,0:T(8,128)}, u32[]{:S(2)}) copy-start(f32[512,1280]{1,0:T(8,128)} %get-tuple-element.43) | copy-start | bytes 7864324
  95.1 8.4 %collective-permute-start.7 = (bf16[2,2,2,80,1280]{4,3,2,1,0:T(8,128)(2,1)S(1)}, bf16[2,2,2,80,1280]{4,3,2,1,0:T(8,128)(2,1)S(1)}, u32[]{:S(2)}, u32[]{:S(2)}) collective-permute-start(bf16[2,2,2,80,1280]{4,3,2,1,0:T(8,128)(2,1)S(1)} %dynamic-slice_bitcast_fusion), channel_id=1, source_target_pairs={{0,2},{2,0},{4,6},{6,4},{8,10},{10,8},{12,14},{14,12},{16,18},{18,... | collective-permute-start | bytes 4915208 | tf_op jit(solution)/shard_map/ppermute | solution.py:83
  101.1 17.6 %collective-permute-start.4 = (f32[15,1280]{1,0:T(8,128)S(1)}, f32[15,1280]{1,0:T(8,128)S(1)}, u32[]{:S(2)}, u32[]{:S(2)}) collective-permute-start(f32[15,1280]{1,0:T(8,128)S(1)} %slice_select_fusion), channel_id=1, source_target_pairs={{0,1},{1,0},{2,3},{3,2},{4,5},{5,4},{6,7},{7,6},{8,9},{9,8},{10,11... | collective-permute-start | bytes 230408 | tf_op jit(solution)/shard_map/ppermute | solution.py:83
  102.6 31.9 %collective-permute-start.22 = (f32[16,1280]{1,0:T(8,128)S(1)}, f32[16,1280]{1,0:T(8,128)S(1)}, u32[]{:S(2)}, u32[]{:S(2)}) collective-permute-start(f32[16,1280]{1,0:T(8,128)S(1)} %slice.297), channel_id=1, source_target_pairs={{0,1},{1,0},{2,3},{3,2},{4,5},{5,4},{6,7},{7,6},{8,9},{9,8},{10,11... | collective-permute-start | bytes 245768 | tf_op jit(solution)/shard_map/ppermute | solution.py:23
  118.5 1.5 collective-permute-start.9
  120.0 7.1 %collective-permute-start.10 = (f32[32,1280]{1,0:T(8,128)S(1)}, f32[32,1280]{1,0:T(8,128)S(1)}, u32[]{:S(2)}, u32[]{:S(2)}) collective-permute-start(f32[32,1280]{1,0:T(8,128)S(1)} %add.259), channel_id=1, source_target_pairs={{0,4},{2,6},{4,0},{6,2},{8,12},{10,14},{12,8},{14,10},{16,20},{18,... | collective-permute-start | bytes 491528 | tf_op jit(solution)/shard_map/ppermute | solution.py:64
  120.7 23.2 %collective-permute-start.8 = (bf16[2,2,80,1280]{3,2,1,0:T(8,128)(2,1)S(1)}, bf16[2,2,80,1280]{3,2,1,0:T(8,128)(2,1)S(1)}, u32[]{:S(2)}, u32[]{:S(2)}) collective-permute-start(bf16[2,2,80,1280]{3,2,1,0:T(8,128)(2,1)S(1)} %dynamic-slice_bitcast_fusion.1), channel_id=1, source_target_pairs={{0,4},{2,6},{4,0},{6,2},{8,12},{10,14},{12,8},{14,10},{16,20},{18,... | collective-permute-start | bytes 2457608 | tf_op jit(solution)/shard_map/ppermute | solution.py:83
  127.2 5.4 %collective-permute-start.11 = (f32[32,1280]{1,0:T(8,128)S(1)}, f32[32,1280]{1,0:T(8,128)S(1)}, u32[]{:S(2)}, u32[]{:S(2)}) collective-permute-start(f32[32,1280]{1,0:T(8,128)S(1)} %add.260), channel_id=1, source_target_pairs={{0,8},{2,10},{4,12},{6,14},{8,0},{10,2},{12,4},{14,6},{16,24},{18,... | collective-permute-start | bytes 491528 | tf_op jit(solution)/shard_map/ppermute | solution.py:64
  130.6 21.2 %collective-permute-start.6 = (bf16[2,2,2,80,640]{4,3,0,1,2:T(8,128)(2,1)S(1)}, bf16[2,2,2,80,640]{4,3,0,1,2:T(8,128)(2,1)S(1)}, u32[]{:S(2)}, u32[]{:S(2)}) collective-permute-start(bf16[2,2,2,80,640]{4,3,0,1,2:T(8,128)(2,1)S(1)} %constant_dynamic-slice_fusion.1), channel_id=1, source_target_pairs={{0,1},{1,0},{2,3},{3,2},{4,5},{5,4},{6,7},{7,6},{8,9},{9,8},{10,11... | collective-permute-start | bytes 2457608 | tf_op jit(solution)/shard_map/ppermute | solution.py:83
  132.6 8.2 %collective-permute-start.12 = (f32[32,1280]{1,0:T(8,128)S(1)}, f32[32,1280]{1,0:T(8,128)S(1)}, u32[]{:S(2)}, u32[]{:S(2)}) collective-permute-start(f32[32,1280]{1,0:T(8,128)S(1)} %add.261), channel_id=1, source_target_pairs={{0,16},{2,18},{4,20},{6,22},{8,24},{10,26},{12,28},{14,30},{16,0},... | collective-permute-start | bytes 491528 | tf_op jit(solution)/shard_map/ppermute | solution.py:64
  140.8 14.5 %collective-permute-start.13 = (f32[32,1280]{1,0:T(8,128)S(1)}, f32[32,1280]{1,0:T(8,128)S(1)}, u32[]{:S(2)}, u32[]{:S(2)}) collective-permute-start(f32[32,1280]{1,0:T(8,128)S(1)} %add.262), channel_id=1, source_target_pairs={{0,1},{1,0},{2,3},{3,2},{4,5},{5,4},{6,7},{7,6},{8,9},{9,8},{10,11... | collective-permute-start | bytes 491528 | tf_op jit(solution)/shard_map/ppermute | solution.py:64
  144.1 11.2 %copy-start.4 = (f32[31,1280]{1,0:T(8,128)S(1)}, f32[31,1280]{1,0:T(8,128)}, u32[]{:S(2)}) copy-start(f32[31,1280]{1,0:T(8,128)} %param.9) | copy-start | bytes 476164
  144.2 22.4 %collective-permute-start.18 = (bf16[2,2,80,640]{3,2,1,0:T(8,128)(2,1)S(1)}, bf16[2,2,80,640]{3,2,1,0:T(8,128)(2,1)S(1)}, u32[]{:S(2)}, u32[]{:S(2)}) collective-permute-start(bf16[2,2,80,640]{3,2,1,0:T(8,128)(2,1)S(1)} %constant_dynamic-slice_fusion), channel_id=1, source_target_pairs={{0,1},{1,0},{2,3},{3,2},{4,5},{5,4},{6,7},{7,6},{8,9},{9,8},{10,11... | collective-permute-start | bytes 1228808 | tf_op jit(solution)/shard_map/ppermute | solution.py:83
  152.1 15.4 %collective-permute-start.14 = (bf16[2,2,80,640]{3,2,0,1:T(8,128)(2,1)S(1)}, bf16[2,2,80,640]{3,2,0,1:T(8,128)(2,1)S(1)}, u32[]{:S(2)}, u32[]{:S(2)}) collective-permute-start(bf16[2,2,80,640]{3,2,0,1:T(8,128)(2,1)S(1)} %dynamic-slice_bitcast_fusion.2), channel_id=1, source_target_pairs={{0,4},{2,6},{4,0},{6,2},{8,12},{10,14},{12,8},{14,10},{16,20},{18,... | collective-permute-start | bytes 1228808 | tf_op jit(solution)/shard_map/ppermute | solution.py:83
  166.8 7.9 %collective-permute-start.19 = (bf16[2,80,640]{2,1,0:T(8,128)(2,1)S(1)}, bf16[2,80,640]{2,1,0:T(8,128)(2,1)S(1)}, u32[]{:S(2)}, u32[]{:S(2)}) collective-permute-start(bf16[2,80,640]{2,1,0:T(8,128)(2,1)S(1)} %dynamic-slice_bitcast_fusion.3), channel_id=1, source_target_pairs={{0,8},{2,10},{4,12},{6,14},{8,0},{10,2},{12,4},{14,6},{16,24},{18,... | collective-permute-start | bytes 614408 | tf_op jit(solution)/shard_map/ppermute | solution.py:83
  167.6 9.2 %collective-permute-start.15 = (bf16[2,80,640]{2,1,0:T(8,128)(2,1)S(1)}, bf16[2,80,640]{2,1,0:T(8,128)(2,1)S(1)}, u32[]{:S(2)}, u32[]{:S(2)}) collective-permute-start(bf16[2,80,640]{2,1,0:T(8,128)(2,1)S(1)} %dynamic-slice_bitcast_fusion.4), channel_id=1, source_target_pairs={{0,8},{2,10},{4,12},{6,14},{8,0},{10,2},{12,4},{14,6},{16,24},{18,... | collective-permute-start | bytes 614408 | tf_op jit(solution)/shard_map/ppermute | solution.py:83
  174.7 5.8 %collective-permute-start.20 = (bf16[80,640]{1,0:T(8,128)(2,1)S(1)}, bf16[80,640]{1,0:T(8,128)(2,1)S(1)}, u32[]{:S(2)}, u32[]{:S(2)}) collective-permute-start(bf16[80,640]{1,0:T(8,128)(2,1)S(1)} %dynamic-slice_bitcast_fusion.5), channel_id=1, source_target_pairs={{0,16},{2,18},{4,20},{6,22},{8,24},{10,26},{12,28},{14,30},{16,0},... | collective-permute-start | bytes 307208 | tf_op jit(solution)/shard_map/ppermute | solution.py:83
  176.9 6.7 %collective-permute-start.16 = (bf16[80,640]{1,0:T(8,128)(2,1)S(1)}, bf16[80,640]{1,0:T(8,128)(2,1)S(1)}, u32[]{:S(2)}, u32[]{:S(2)}) collective-permute-start(bf16[80,640]{1,0:T(8,128)(2,1)S(1)} %dynamic-slice_bitcast_fusion.6), channel_id=1, source_target_pairs={{0,16},{2,18},{4,20},{6,22},{8,24},{10,26},{12,28},{14,30},{16,0},... | collective-permute-start | bytes 307208 | tf_op jit(solution)/shard_map/ppermute | solution.py:83
  180.6 4.7 %collective-permute-start.21 = (bf16[80,640]{1,0:T(8,128)(2,1)S(1)}, bf16[80,640]{1,0:T(8,128)(2,1)S(1)}, u32[]{:S(2)}, u32[]{:S(2)}) collective-permute-start(bf16[80,640]{1,0:T(8,128)(2,1)S(1)} %fusion.41), channel_id=1, source_target_pairs={{0,1},{1,0},{2,3},{3,2},{4,5},{5,4},{6,7},{7,6},{8,9},{9,8},{10,11... | collective-permute-start | bytes 307208 | tf_op jit(solution)/shard_map/ppermute | solution.py:83
  183.6 4.7 %collective-permute-start.17 = (bf16[80,640]{1,0:T(8,128)(2,1)S(1)}, bf16[80,640]{1,0:T(8,128)(2,1)S(1)}, u32[]{:S(2)}, u32[]{:S(2)}) collective-permute-start(bf16[80,640]{1,0:T(8,128)(2,1)S(1)} %fusion.42), channel_id=1, source_target_pairs={{0,1},{1,0},{2,3},{3,2},{4,5},{5,4},{6,7},{7,6},{8,9},{9,8},{10,11... | collective-permute-start | bytes 307208 | tf_op jit(solution)/shard_map/ppermute | solution.py:83
Sparse Core Ops, SparseCore 0:
  10.3 66.0 all-gather.1
